TPU v7x, 32 devices: a whole 2x2x4 slice. The times are simulated.
32 devices in a mesh: leaf: 8 (over z, y), rows: 4 (over x, core).
Axes of the slice: x: 2, y: 2, z: 4, core: 2. Of those that a mesh axis runs over, the one named last changes fastest.
Arguments:
- samples: bfloat16 [262144, 256], P(('leaf', 'rows')), may hold values from -40 to 40
- row_order: int32 [2048, 128], P(('leaf', 'rows')), may hold values from 0 to 127, each once within a row
- cluster_map: int32 [2048], P(('leaf', 'rows')), may hold values from 0 to 7, as said below
- leaf_sketch: bfloat16 [256, 128], replicated, may hold values from -0.375 to 0.375
- level_sketch: float32 [3, 256, 128], replicated, may hold values from -0.375 to 0.375
Outputs:
- bases: bfloat16 [524288, 128], P(('leaf', 'rows'))
- transfers: float32 [8, 3, 128, 128], P('leaf')
- summaries: float32 [8, 128, 256], P('leaf')
Inputs may be any that keep to these rules, and one draw needn't show every extreme that they name: `cluster_map`: the 64 blocks of one device name each cluster at most 16 times; in every draw one cluster is named exactly 16 times on every device.
All inputs are finite; a program needn't handle non-finite values.
Results may differ from a plain program's by a relative error of at most 0.023.
Values may be sent and summed in bfloat16 or wider, within the bound.
A program may use at most 128 MiB of HBM per device.

v0:
```python
import math

import jax
import jax.numpy as jnp
from jax import lax
from jax.sharding import PartitionSpec as P

LEVELS = 3


SHIFT = 0.01


def from_partner(value, axis, distance):
    mask = 2**distance
    pairs = [(source, source ^ mask) for source in range(lax.axis_size(axis))]
    return lax.ppermute(value, axis, pairs)


def merge_pair(stacked, sketch_level):
    rows_total = stacked.shape[0]
    rank_cols = sketch_level.shape[1]
    sample_cols = stacked.shape[1]
    projected = jnp.dot(stacked, sketch_level, precision=lax.Precision.HIGHEST)
    gram = jnp.dot(
        projected.T, projected, precision=lax.Precision.HIGHEST
    ) / rows_total + SHIFT * jnp.eye(rank_cols, dtype=jnp.float32)
    lower_factor = jnp.linalg.cholesky(gram)
    inverse_lower = lax.linalg.triangular_solve(
        lower_factor, jnp.eye(rank_cols, dtype=jnp.float32), left_side=True, lower=True
    )
    transfer = jnp.dot(projected, inverse_lower.T, precision=lax.Precision.HIGHEST)
    product = jnp.dot(projected.T, stacked, precision=lax.Precision.HIGHEST)
    parent = jnp.dot(inverse_lower, product, precision=lax.Precision.HIGHEST) * (
        math.sqrt(sample_cols) / rows_total
    )
    return (transfer, parent)


def split_apply(sketched, inverse_lower):
    whole = inverse_lower.T
    upper_part = whole.astype(jnp.bfloat16)
    lower_part = (whole - upper_part.astype(jnp.float32)).astype(jnp.bfloat16)
    first = jnp.dot(sketched, upper_part, preferred_element_type=jnp.float32)
    second = jnp.dot(sketched, lower_part, preferred_element_type=jnp.float32)
    return (first + second).astype(jnp.bfloat16)


def body(samples, row_order, cluster_map, leaf_sketch, level_sketch):
    block_count = cluster_map.shape[0]
    block_rows = row_order.shape[1]
    sample_cols = samples.shape[1]
    rank_cols = leaf_sketch.shape[1]
    clusters = lax.axis_size("leaf")
    capacity = 2 * block_count // clusters
    blocks = samples.reshape(block_count, block_rows, sample_cols)
    ordered = jnp.take_along_axis(blocks, row_order[:, :, None], axis=1)
    hits = (cluster_map[:, None] == jnp.arange(clusters, dtype=jnp.int32)[None, :]).astype(
        jnp.int32
    )
    before = jnp.cumsum(hits, axis=0) - hits
    slot_rank = jnp.sum(before * hits, axis=1)
    slot_index = cluster_map * capacity + slot_rank
    placing = (
        slot_index[:, None] == jnp.arange(clusters * capacity, dtype=jnp.int32)[None, :]
    ).astype(jnp.bfloat16)
    flat_rows = ordered.reshape(block_count, block_rows * sample_cols)
    packed = jnp.einsum("sk,sr->kr", placing, flat_rows, preferred_element_type=jnp.float32).astype(
        jnp.bfloat16
    )
    packed = packed.reshape(clusters, capacity * block_rows, sample_cols)
    received = lax.all_to_all(packed, "leaf", split_axis=0, concat_axis=0, tiled=True).reshape(
        -1, sample_cols
    )
    sketched = jnp.dot(received, leaf_sketch, preferred_element_type=jnp.float32).astype(
        jnp.bfloat16
    )
    contract = (((0,), (0,)), ((), ()))
    gram_part = lax.dot_general(sketched, sketched, contract, preferred_element_type=jnp.float32)
    cross_part = lax.dot_general(sketched, received, contract, preferred_element_type=jnp.float32)
    gram_total, cross_total = lax.psum((gram_part, cross_part), "rows")
    row_norm = float(lax.axis_size("rows") * block_count * block_rows)
    gram_total = gram_total / row_norm + SHIFT * jnp.eye(rank_cols, dtype=jnp.float32)
    lower_factor = jnp.linalg.cholesky(gram_total)
    inverse_lower = lax.linalg.triangular_solve(
        lower_factor, jnp.eye(rank_cols, dtype=jnp.float32), left_side=True, lower=True
    )
    basis = split_apply(sketched, inverse_lower)
    summary = jnp.dot(inverse_lower, cross_total, precision=lax.Precision.HIGHEST) * (
        math.sqrt(sample_cols) / row_norm
    )
    my_index = lax.axis_index("leaf")
    halves = []
    group_nodes = summary[None]
    for depth_index in range(LEVELS):
        partner_nodes = from_partner(group_nodes, "leaf", depth_index)
        side_bit = my_index >> depth_index & 1
        group_nodes = jnp.where(
            side_bit == 0,
            jnp.concatenate([group_nodes, partner_nodes], axis=0),
            jnp.concatenate([partner_nodes, group_nodes], axis=0),
        )
    group_size = 2**LEVELS
    local_index = my_index % group_size
    nodes_now = group_nodes
    for depth_index in range(LEVELS):
        paired = nodes_now.reshape(-1, 2 * rank_cols, sample_cols)
        transfer_all, parent_all = jax.vmap(merge_pair, in_axes=(0, None))(
            paired, level_sketch[depth_index]
        )
        chosen = lax.dynamic_index_in_dim(
            transfer_all, local_index >> depth_index + 1, 0, keepdims=False
        )
        side_bit = local_index >> depth_index & 1
        halves.append(lax.dynamic_slice_in_dim(chosen, side_bit * rank_cols, rank_cols, 0))
        nodes_now = parent_all
    summary = nodes_now[0]
    return (basis, jnp.stack(halves, axis=0)[None], summary[None])


def solution(mesh):
    in_specs = (P(("leaf", "rows"), None), P(("leaf", "rows"), None), P(("leaf", "rows")), P(), P())
    out_specs = (P(("leaf", "rows"), None), P("leaf", None, None, None), P("leaf", None, None))
    return jax.shard_map(body, mesh=mesh, in_specs=in_specs, out_specs=out_specs, check_vma=False)
```

profile of v0, /device:TPU:0, one launch (start us, length us, event | category | flops | bytes accessed | tf_op | source)
XLA Modules:
  0.0 650.4 jit_solution(659209589816532234)
XLA Ops:
  7.2 0.8 fusion.36
  8.0 0.8 compare_and_fusion
  8.8 143.3 %gather_fusion = bf16[8192,256]{1,0:T(8,128)(2,1)} fusion(bf16[64,128,256]{2,1,0:T(8,128)(2,1)} %bitcast.132, s32[8192]{0:T(1024)S(1)} %fusion.36), kind=kCustom, calls=%fused_computation | custom fusion | bytes 8454144 | tf_op jit(solution)/shard_map/jit(take_along_axis)/gather | solution.py:57
  152.1 4.4 broadcast_select_fusion
  156.5 4.6 copy.64
  161.4 7.8 %convolution_convert_fusion = bf16[128,32768]{1,0:T(8,128)(2,1)} fusion(bf16[64,32768]{1,0:T(8,128)(2,1)} %bitcast.135, s32[64]{0:T(128)S(1)} %multiply_add_fusion.1), kind=kOutput, calls=%fused_computation.1 | convolution fusion | flops 541073408 | bytes 12583168 | tf_op jit(solution)/shard_map/sk,sr->kr/dot_general | solution.py:68
  169.3 13.5 %reshape.175 = bf16[8,2048,256]{2,1,0:T(8,128)(2,1)} reshape(bf16[128,32768]{1,0:T(8,128)(2,1)} %convolution_convert_fusion) | data formatting | bytes 16777216 | tf_op jit(solution)/shard_map/reshape | solution.py:71
  182.8 7.3 %all-to-all-start = ((bf16[8,2048,256]{2,1,0:T(8,128)(2,1)}), bf16[8,2048,256]{2,1,0:T(8,128)(2,1)}, u32[]{:S(2)}, u32[]{:S(2)}) async-start(bf16[8,2048,256]{2,1,0:T(8,128)(2,1)} %reshape.175), calls=%async_computation | async-start | bytes 16777216 | tf_op jit(solution)/shard_map/all_to_all | solution.py:72
  190.3 182.9 %all-to-all-done = bf16[8,2048,256]{2,1,0:T(8,128)(2,1)} async-done(((bf16[8,2048,256]{2,1,0:T(8,128)(2,1)}), bf16[8,2048,256]{2,1,0:T(8,128)(2,1)}, u32[]{:S(2)}, u32[]{:S(2)}) %all-to-all-start) | async-done | bytes 8388640 | tf_op jit(solution)/shard_map/all_to_all | solution.py:72
  373.2 5.7 convolution_convert_fusion.1
  378.9 2.0 fusion.44
  381.0 5.7 fusion.45
  386.8 30.9 %all-reduce.3.cloned.1.call-done = (f32[128,128]{0,1:T(8,128)}, f32[128,256]{1,0:T(8,128)}) async-done(((f32[128,128]{0,1:T(8,128)}, f32[128,256]{1,0:T(8,128)}), (f32[128,128]{0,1:T(8,128)}, f32[128,256]{1,0:T(8,128)})) %all-reduce.3.cloned.1.call-update) | async-done | bytes 196624 | tf_op jit(solution)/shard_map/psum | solution.py:81
  417.7 0.9 multiply_add_fusion
  418.6 0.9 fusion.30
  419.6 11.7 %cholesky.63 = f32[128,128]{1,0:T(8,128)S(1)} custom-call(f32[128,128]{1,0:T(8,128)S(1)} %copy.34), custom_call_target="Cholesky" | custom-call | tf_op jit(solution)/shard_map/jit(cholesky)/cholesky | solution.py:84
  431.5 0.6 compare_reduce_fusion.3
  432.2 0.7 fusion.22
  432.9 9.8 %custom-call.27 = f32[1,128,128]{1,2,0:T(8,128)S(1)} custom-call(f32[1,128,128]{2,1,0:T(8,128)S(1)} %copy.37), custom_call_target="InvertDiagBlocksLowerTriangular" | custom-call | tf_op jit(solution)/shard_map/triangular_solve | solution.py:85
  443.0 1.2 fusion.2
  444.2 1.5 collective-permute-start
  446.3 2.9 collective-permute-done
  449.3 1.6 collective-permute-start.1
  450.8 3.9 fusion.41
  454.7 1.0 collective-permute-done.1
  455.8 3.1 collective-permute-start.2
  458.9 3.3 fusion
  462.2 16.1 %collective-permute-done.2 = f32[4,128,256]{2,1,0:T(8,128)S(1)} collective-permute-done((f32[4,128,256]{2,1,0:T(8,128)S(1)}, f32[4,128,256]{2,1,0:T(8,128)S(1)}, u32[]{:S(2)}, u32[]{:S(2)}) %collective-permute-start.2) | collective-permute-done | bytes 524320 | tf_op jit(solution)/shard_map/ppermute | solution.py:17
  478.3 1.0 fusion.16
  479.3 1.1 fusion.47
  480.4 1.1 broadcast_add_fusion
  481.6 46.9 %custom-call.28 = f32[4,128,128]{2,1,0:T(8,128)S(1)} custom-call(f32[4,128,128]{2,1,0:T(8,128)S(1)} %fusion.7), custom_call_target="Cholesky" | custom-call | tf_op jit(solution)/shard_map/vmap(jit(cholesky))/cholesky | solution.py:28
  528.8 39.3 %custom-call.29 = f32[4,1,128,128]{2,3,1,0:T(8,128)S(1)} custom-call(f32[4,1,128,128]{3,2,1,0:T(8,128)S(1)} %select_bitcast_fusion), custom_call_target="InvertDiagBlocksLowerTriangular" | custom-call | tf_op jit(solution)/shard_map/vmap()/triangular_solve | solution.py:29
  568.1 0.6 fusion.4
  568.7 0.6 convolution_multiply_fusion
  569.3 0.6 fusion.14
  569.9 0.7 broadcast_add_fusion.1
  570.6 0.7 fusion.49
  571.3 0.6 fusion.46
  572.0 23.6 %custom-call.30 = f32[2,128,128]{2,1,0:T(8,128)S(1)} custom-call(f32[2,128,128]{2,1,0:T(8,128)S(1)} %fusion.13), custom_call_target="Cholesky" | custom-call | tf_op jit(solution)/shard_map/vmap(jit(cholesky))/cholesky | solution.py:28
  595.9 19.9 %custom-call.31 = f32[2,1,128,128]{2,3,1,0:T(8,128)S(1)} custom-call(f32[2,1,128,128]{3,2,1,0:T(8,128)S(1)} %select_bitcast_fusion.1), custom_call_target="InvertDiagBlocksLowerTriangular" | custom-call | tf_op jit(solution)/shard_map/vmap()/triangular_solve | solution.py:29
  617.7 0.4 fusion.51
  618.2 11.7 %custom-call.32 = f32[1,128,128]{2,1,0:T(8,128)S(1)} custom-call(f32[1,128,128]{2,1,0:T(8,128)S(1)} %fusion.24), custom_call_target="Cholesky" | custom-call | tf_op jit(solution)/shard_map/vmap(jit(cholesky))/cholesky | solution.py:28
  630.0 0.6 compare_reduce_fusion
  630.6 0.7 fusion.23
  631.3 9.8 %custom-call.33 = f32[1,1,128,128]{2,3,1,0:T(8,128)S(1)} custom-call(f32[1,1,128,128]{3,2,1,0:T(8,128)S(1)} %fusion.23), custom_call_target="InvertDiagBlocksLowerTriangular" | custom-call | tf_op jit(solution)/shard_map/vmap()/triangular_solve | solution.py:29
  641.6 0.9 fusion.1
  642.6 0.7 maximum_bitcast_fusion
  (58 shorter events, 5.4 us)
Async XLA Ops:
  7.2 366.0 %copy-start = (bf16[256,128]{1,0:T(8,128)(2,1)S(1)}, bf16[256,128]{1,0:T(8,128)(2,1)}, u32[]{:S(2)}) copy-start(bf16[256,128]{1,0:T(8,128)(2,1)} %param.8) | copy-start | bytes 196612
  156.4 4.6 copy-start.5
  182.8 190.4 %all-to-all-start = ((bf16[8,2048,256]{2,1,0:T(8,128)(2,1)}), bf16[8,2048,256]{2,1,0:T(8,128)(2,1)}, u32[]{:S(2)}, u32[]{:S(2)}) async-start(bf16[8,2048,256]{2,1,0:T(8,128)(2,1)} %reshape.175), calls=%async_computation | async-start | bytes 16777216 | tf_op jit(solution)/shard_map/all_to_all | solution.py:72
  190.0 227.6 %all-reduce.3.cloned.1.call-start = ((), (), s32[]{:S(2)}) async-start(), calls=%async_computation.1 | async-start | bytes 393216 | tf_op jit(solution)/shard_map/psum | solution.py:81
  378.9 2.0 copy-start.2
  444.2 5.0 collective-permute-start
  449.2 9.7 %copy-start.3 = (bf16[16384,128]{1,0:T(8,128)(2,1)S(1)}, bf16[16384,128]{1,0:T(8,128)(2,1)}, u32[]{:S(2)}) copy-start(bf16[16384,128]{1,0:T(8,128)(2,1)} %copy-done.2) | copy-start | bytes 12582916
  449.3 6.4 collective-permute-start.1
  455.7 22.6 %copy-start.4 = (f32[3,256,128]{2,1,0:T(8,128)S(1)}, f32[3,256,128]{2,1,0:T(8,128)}, u32[]{:S(2)}) copy-start(f32[3,256,128]{2,1,0:T(8,128)} %param.9) | copy-start | bytes 1179652
  455.8 22.5 %collective-permute-start.2 = (f32[4,128,256]{2,1,0:T(8,128)S(1)}, f32[4,128,256]{2,1,0:T(8,128)S(1)}, u32[]{:S(2)}, u32[]{:S(2)}) collective-permute-start(f32[4,128,256]{2,1,0:T(8,128)S(1)} %maximum_select_fusion.1), channel_id=1, source_target_pairs={{0,16},{4,20},{8,24},{12,28},{16,0},{20,4},{24,8},{28,12},{1,17},{... | collective-permute-start | bytes 1572872 | tf_op jit(solution)/shard_map/ppermute | solution.py:17
  569.9 73.4 %copy-start.1 = (bf16[256,128]{1,0:T(8,128)(2,1)S(1)}, bf16[256,128]{1,0:T(8,128)(2,1)}, u32[]{:S(2)}) copy-start(bf16[256,128]{1,0:T(8,128)(2,1)} %param.8) | copy-start | bytes 196612
Sparse Core Ops, SparseCore 0:
  386.9 30.7 all-reduce.2
where the time goes:
time: 658 us; the launch traced here: 650 us
  waiting for transfers between devices  234 us (36%)
  other arithmetic  185 us (28%)
  local copies, waits for them, and re-layouts  163 us (25%)
  matrix products  40.4 us (6%)
  between operations  14.8 us (2%)
  starting transfers between devices  13.8 us (2%)
    all_to_all x1, waiting for transfers between devices, body(): lax.all_to_all(packed, 'leaf', split_axis=0, concat_axis=0, tiled=True)  183 us
    gather x1, local copies, waits for them, and re-layouts, body(): ordered = jnp.take_along_axis(blocks, row_order[:, :, None], axis=1)  143 us
    another operation x9, other arithmetic, merge_pair(): lower_factor = jnp.linalg.cholesky(gram)  83.2 us
    another operation x6, other arithmetic, merge_pair(): lax.linalg.triangular_solve(lower_factor, jnp.eye(rank_cols, dtype=jnp.fl...  69.9 us
    psum x1, waiting for transfers between devices, body(): gram_total, cross_total = lax.psum((gram_part, cross_part), 'rows')  30.9 us
    ppermute x3, waiting for transfers between devices, from_partner(): return lax.ppermute(value, axis, pairs)  20 us
    reshape x1, local copies, waits for them, and re-layouts, body(): packed = packed.reshape(clusters, capacity * block_rows, sample_cols)  13.5 us
  transfers between devices with their start and end apart: 5, of which 5 were waited for; matrix products, arithmetic and copies ran while one was open for 1% of the time, Pallas kernels for 0%

commit v1 on v0

v1 whole, which is shorter than its diff:
```python
import functools
import math

import jax
import jax.numpy as jnp
from jax import lax
from jax.experimental import pallas as pl
from jax.experimental.pallas import tpu as pltpu
from jax.sharding import PartitionSpec as P

LEVELS = 3
SHIFT = 0.01
TILE = 8
GROUP = 4
STEP_BLOCKS = 8
VMEM_BYTES = 56 * 1024 * 1024
MESH = pl.DeviceIdType.MESH
HIGHEST = lax.Precision.HIGHEST


def dot_first(left, right, precision=None):
    return lax.dot_general(
        left,
        right,
        (((0,), (0,)), ((), ())),
        precision=precision,
        preferred_element_type=jnp.float32,
    )


def dot_last(left, right, precision=None):
    return lax.dot_general(
        left,
        right,
        (((1,), (1,)), ((), ())),
        precision=precision,
        preferred_element_type=jnp.float32,
    )


def identity(size):
    rows = lax.broadcasted_iota(jnp.int32, (size, size), 0)
    cols = lax.broadcasted_iota(jnp.int32, (size, size), 1)
    return jnp.where(rows == cols, 1.0, 0.0).astype(jnp.float32)


def inverse_factor(gram):
    size = gram.shape[0]
    row_id = lax.broadcasted_iota(jnp.int32, (size, size), 0)

    def panel(_, carry):
        a, b = carry
        for s in range(0, TILE, GROUP):
            cols = [jnp.broadcast_to(a[:, s + j : s + j + 1], (size, size)) for j in range(GROUP)]
            rows_a = [a[s + j : s + j + 1, :] for j in range(GROUP)]
            rows_b = [b[s + j : s + j + 1, :] for j in range(GROUP)]
            scales = []
            for j in range(GROUP):
                pivot = cols[j][s + j : s + j + 1, :]
                inv = 1.0 / pivot
                scales.append(lax.rsqrt(pivot))
                for i in range(j + 1, GROUP):
                    factor = cols[j][s + i : s + i + 1, :] * inv
                    cols[i] = cols[i] - cols[j] * factor
                    rows_a[i] = rows_a[i] - factor * rows_a[j]
                    rows_b[i] = rows_b[i] - factor * rows_b[j]
                below = jnp.where(row_id > s + j, cols[j], 0.0)
                a = a - below * (rows_a[j] * inv)
                b = b - below * (rows_b[j] * inv)
            for j in range(GROUP):
                b = jnp.where(row_id == s + j, rows_b[j] * scales[j], b)
        a = jnp.concatenate([a[TILE:], jnp.zeros((TILE, size), jnp.float32)], axis=0)
        a = pltpu.roll(a, size - TILE, 1)
        b = jnp.concatenate([b[TILE:], b[:TILE]], axis=0)
        return a, b

    return lax.fori_loop(0, size // TILE, panel, (gram, identity(size)))[1]


def local_kernel(capacity, map_ref, order_ref, x_ref, sketch_ref, packed_ref, sums_ref, count_ref):
    step = pl.program_id(0)
    clusters = sums_ref.shape[0]
    rows = order_ref.shape[1]

    @pl.when(step == 0)
    def _():
        def clear(c, carry):
            count_ref[c] = 0
            sums_ref[c] = jnp.zeros(sums_ref.shape[1:], jnp.float32)
            for j in range(capacity):
                packed_ref[c * capacity + j] = jnp.zeros(packed_ref.shape[1:], jnp.bfloat16)
            return carry

        lax.fori_loop(0, clusters, clear, 0)

    sketched = jnp.dot(x_ref[...], sketch_ref[...], preferred_element_type=jnp.float32).astype(
        jnp.bfloat16
    )
    source = lax.broadcasted_iota(jnp.int32, (rows, rows), 0)
    for i in range(STEP_BLOCKS):
        cluster = map_ref[step * STEP_BLOCKS + i]
        rank = count_ref[cluster]
        count_ref[cluster] = rank + 1
        block = sketched[i * rows : (i + 1) * rows]
        taken = jnp.where(source == order_ref[i : i + 1, :], 1.0, 0.0).astype(jnp.bfloat16)
        packed_ref[cluster * capacity + rank] = dot_first(taken, block).astype(jnp.bfloat16)
        wide = jnp.concatenate([block, x_ref[i * rows : (i + 1) * rows, :]], axis=1)
        sums_ref[cluster] += dot_first(block, wide)


def flip(index, mask):
    return index + mask - 2 * mask * lax.rem(lax.div(index, mask), 2)


def exchange_kernel(
    capacity,
    row_norm,
    leaves,
    lines,
    packed_ref,
    sums_ref,
    level_ref,
    received_ref,
    inverse_ref,
    transfers_ref,
    summary_ref,
    *scratch,
):
    rounds = lines.bit_length() - 1
    halves = scratch[:rounds]
    partial = scratch[rounds : 2 * rounds]
    (
        landed,
        whole,
        nodes,
        siblings,
        block_send,
        block_recv,
        half_send,
        half_recv,
        leaf_send,
        leaf_recv,
        line_send,
        line_recv,
        node_send,
        node_recv,
        own_sem,
    ) = scratch[2 * rounds :]
    me = lax.axis_index("leaf")
    line = lax.axis_index("rows")
    rank = inverse_ref.shape[0]
    sample_cols = level_ref.shape[1]

    barrier = pltpu.get_barrier_semaphore()
    for d in range(1, leaves):
        pl.semaphore_signal(
            barrier, inc=1, device_id=(lax.rem(me + d, leaves), line), device_id_type=MESH
        )
    for d in range(1, lines):
        pl.semaphore_signal(
            barrier, inc=1, device_id=(me, lax.rem(line + d, lines)), device_id_type=MESH
        )
    pl.semaphore_wait(barrier, leaves + lines - 2)

    def remote(src, dst, send, recv, target):
        copy = pltpu.make_async_remote_copy(
            src_ref=src,
            dst_ref=dst,
            send_sem=send,
            recv_sem=recv,
            device_id=target,
            device_id_type=MESH,
        )
        copy.start()
        return copy

    held, start, size = sums_ref, 0, rank
    for k in range(rounds):
        mask = 2**k
        size //= 2
        side = lax.rem(lax.div(line, mask), 2)
        copy = remote(
            held.at[:, pl.ds(pl.multiple_of((1 - side) * size, size), size), :],
            halves[k],
            half_send.at[k],
            half_recv.at[k],
            (me, flip(line, mask)),
        )
        if k == 0:
            own = pltpu.make_async_copy(
                packed_ref.at[pl.ds(me * capacity, capacity)],
                received_ref.at[pl.ds(me * capacity, capacity)],
                own_sem,
            )
            own.start()
        copy.wait()
        kept = pl.multiple_of(side * size, size)
        for c in range(leaves):
            partial[k][c] = held[c, pl.ds(kept, size), :] + halves[k][c]
        held, start = partial[k], start + side * size

    sums = []
    for d in range(1, leaves):
        peer = lax.rem(me + d, leaves)
        sums.append(
            remote(held.at[peer], landed.at[me], leaf_send.at[d], leaf_recv.at[d], (peer, line))
        )
    blocks = []
    for d in sorted(range(1, leaves), key=lambda value: abs(value - leaves // 2)):
        peer = lax.rem(me + d, leaves)
        blocks.append(
            remote(
                packed_ref.at[pl.ds(peer * capacity, capacity)],
                received_ref.at[pl.ds(me * capacity, capacity)],
                block_send.at[d],
                block_recv.at[d],
                (peer, line),
            )
        )
    total = held[me]
    for d in range(1, leaves):
        sums[d - 1].wait()
        total = total + landed[lax.rem(me - d + leaves, leaves)]
    start = pl.multiple_of(start, size)
    whole[pl.ds(start, size), :] = total
    shares = [
        remote(
            whole.at[pl.ds(start, size), :],
            whole.at[pl.ds(start, size), :],
            line_send.at[d],
            line_recv.at[d],
            (me, lax.rem(line + d, lines)),
        )
        for d in range(1, lines)
    ]
    for copy in shares:
        copy.wait()

    eye = identity(rank)
    inverse = inverse_factor(whole[:, :rank] / row_norm + SHIFT * eye)
    inverse_ref[...] = inverse
    nodes[0] = jnp.dot(inverse, whole[:, rank:], precision=HIGHEST) * (
        math.sqrt(sample_cols) / row_norm
    )
    for t in range(LEVELS):
        copy = remote(
            nodes.at[t], siblings.at[t], node_send.at[t], node_recv.at[t], (flip(me, 2**t), line)
        )
        own_node = nodes[t]
        sketch = level_ref[t]
        projected = jnp.dot(own_node, sketch, precision=HIGHEST)
        wide = jnp.concatenate([projected, own_node], axis=1)
        own_product = dot_first(projected, wide, HIGHEST)
        copy.wait()
        other_node = siblings[t]
        other = jnp.dot(other_node, sketch, precision=HIGHEST)
        other_wide = jnp.concatenate([other, other_node], axis=1)
        product = own_product + dot_first(other, other_wide, HIGHEST)
        inverse = inverse_factor(product[:, :rank] / (2 * rank) + SHIFT * eye)
        transfers_ref[t] = dot_last(projected, inverse, HIGHEST)
        parent = jnp.dot(inverse, product[:, rank:], precision=HIGHEST) * (
            math.sqrt(sample_cols) / (2 * rank)
        )
        if t == LEVELS - 1:
            summary_ref[...] = parent
        else:
            nodes[t + 1] = parent

    own.wait()
    for copy in blocks:
        copy.wait()


def basis_kernel(rows_ref, inverse_ref, basis_ref):
    inverse = inverse_ref[...]
    upper = inverse.astype(jnp.bfloat16)
    lower = (inverse - upper.astype(jnp.float32)).astype(jnp.bfloat16)
    rows = rows_ref[...]
    basis_ref[...] = (dot_last(rows, upper) + dot_last(rows, lower)).astype(jnp.bfloat16)


def body(samples, row_order, cluster_map, leaf_sketch, level_sketch):
    block_count = cluster_map.shape[0]
    block_rows = row_order.shape[1]
    sample_cols = samples.shape[1]
    rank = leaf_sketch.shape[1]
    leaves = lax.axis_size("leaf")
    lines = lax.axis_size("rows")
    capacity = 2 * block_count // leaves
    slots = leaves * capacity
    width = rank + sample_cols
    row_norm = float(lines * block_count * block_rows)
    vmem = pl.BlockSpec(memory_space=pltpu.VMEM)
    anywhere = pl.BlockSpec(memory_space=pl.ANY)

    packed, sums = pl.pallas_call(
        functools.partial(local_kernel, capacity),
        grid=(block_count // STEP_BLOCKS,),
        in_specs=[
            pl.BlockSpec(memory_space=pltpu.SMEM),
            pl.BlockSpec((STEP_BLOCKS, block_rows), lambda i: (i, 0)),
            pl.BlockSpec((STEP_BLOCKS * block_rows, sample_cols), lambda i: (i, 0)),
            pl.BlockSpec((sample_cols, rank), lambda i: (0, 0)),
        ],
        out_specs=[
            pl.BlockSpec((slots, block_rows, rank), lambda i: (0, 0, 0)),
            pl.BlockSpec((leaves, rank, width), lambda i: (0, 0, 0)),
        ],
        out_shape=[
            jax.ShapeDtypeStruct((slots, block_rows, rank), jnp.bfloat16),
            jax.ShapeDtypeStruct((leaves, rank, width), jnp.float32),
        ],
        scratch_shapes=[pltpu.SMEM((leaves,), jnp.int32)],
        compiler_params=pltpu.CompilerParams(vmem_limit_bytes=VMEM_BYTES),
        name="sketch_blocks",
    )(cluster_map, row_order, samples, leaf_sketch)

    rounds = lines.bit_length() - 1
    shares = [
        pltpu.VMEM((leaves, rank >> (k + 1), width), jnp.float32) for k in range(rounds)
    ]
    dma = pltpu.SemaphoreType.DMA
    received, inverse, transfers, summary = pl.pallas_call(
        functools.partial(exchange_kernel, capacity, row_norm, leaves, lines),
        in_specs=[anywhere, vmem, vmem],
        out_specs=[anywhere, vmem, vmem, vmem],
        out_shape=[
            jax.ShapeDtypeStruct((slots, block_rows, rank), jnp.bfloat16),
            jax.ShapeDtypeStruct((rank, rank), jnp.float32),
            jax.ShapeDtypeStruct((LEVELS, rank, rank), jnp.float32),
            jax.ShapeDtypeStruct((rank, sample_cols), jnp.float32),
        ],
        scratch_shapes=[
            *shares,
            *shares,
            pltpu.VMEM((leaves, rank // lines, width), jnp.float32),
            pltpu.VMEM((rank, width), jnp.float32),
            pltpu.VMEM((LEVELS, rank, sample_cols), jnp.float32),
            pltpu.VMEM((LEVELS, rank, sample_cols), jnp.float32),
            dma((leaves,)),
            dma((leaves,)),
            dma((rounds,)),
            dma((rounds,)),
            dma((leaves,)),
            dma((leaves,)),
            dma((lines,)),
            dma((lines,)),
            dma((LEVELS,)),
            dma((LEVELS,)),
            dma,
        ],
        compiler_params=pltpu.CompilerParams(
            collective_id=0, has_side_effects=True, vmem_limit_bytes=VMEM_BYTES
        ),
        name="exchange_and_merge",
    )(packed, sums, level_sketch)

    total_rows = slots * block_rows
    tile = min(2048, total_rows)
    basis = pl.pallas_call(
        basis_kernel,
        grid=(total_rows // tile,),
        in_specs=[
            pl.BlockSpec((tile, rank), lambda i: (i, 0)),
            pl.BlockSpec((rank, rank), lambda i: (0, 0)),
        ],
        out_specs=pl.BlockSpec((tile, rank), lambda i: (i, 0)),
        out_shape=jax.ShapeDtypeStruct((total_rows, rank), jnp.bfloat16),
        compiler_params=pltpu.CompilerParams(vmem_limit_bytes=VMEM_BYTES),
        name="leaf_bases",
    )(received.reshape(total_rows, rank), inverse)
    return basis, transfers[None], summary[None]


def solution(mesh):
    in_specs = (P(("leaf", "rows"), None), P(("leaf", "rows"), None), P(("leaf", "rows")), P(), P())
    out_specs = (P(("leaf", "rows"), None), P("leaf", None, None, None), P("leaf", None, None))
    return jax.shard_map(body, mesh=mesh, in_specs=in_specs, out_specs=out_specs, check_vma=False)
```

time: 658 us -> 165 us (0.25); the launches traced: 650 us -> 164 us
  waiting for transfers between devices: 234 us -> 0 us
  other arithmetic: 185 us -> 0 us
  Pallas kernels: 0 us -> 162 us
  local copies, waits for them, and re-layouts: 163 us -> 1.34 us
  matrix products: 40.4 us -> 0 us
  between operations: 14.8 us -> 0.66 us
  starting transfers between devices: 13.8 us -> 0 us
    all_to_all x1 -> x0, waiting for transfers between devices: 183 us -> none  [body(): lax.all_to_all(packed, 'leaf', split_axis=0, concat_axis=0, tiled=True)]
    another operation x23 -> x0, other arithmetic: 176 us -> none  [the longest x9 83.2 us: merge_pair(): lower_factor = jnp.linalg.cholesky(gram)]
    pallas_call x0 -> x3, Pallas kernels: none -> 162 us  [the longest x1 143 us: body(): pl.pallas_call(functools.partial(exchange_kernel, capacity, row_norm, lea...]
    gather x1 -> x0, local copies, waits for them, and re-layouts: 143 us -> none  [body(): ordered = jnp.take_along_axis(blocks, row_order[:, :, None], axis=1)]
    dot_general x22 -> x0, matrix products: 39 us -> none  [the longest x1 7.85 us: body(): jnp.einsum('sk,sr->kr', placing, flat_rows, preferred_element_type=jnp.fl...]
    psum x1 -> x0, waiting for transfers between devices: 30.9 us -> none  [body(): gram_total, cross_total = lax.psum((gram_part, cross_part), 'rows')]
    ppermute x3 -> x0, waiting for transfers between devices: 20 us -> none  [from_partner(): return lax.ppermute(value, axis, pairs)]
    reshape x1 -> x0, local copies, waits for them, and re-layouts: 13.5 us -> none  [body(): packed = packed.reshape(clusters, capacity * block_rows, sample_cols)]
  transfers between devices with their start and end apart: 5 -> 0, of which waited for: 5 -> 0; matrix products, arithmetic and copies ran while one was open for 1% -> 0% of each run, Pallas kernels for 0% -> 0%
where the time goes in v1:
time: 165 us; the launch traced here: 164 us
  Pallas kernels  162 us (98%)
    pallas_call x1, Pallas kernels, body(): pl.pallas_call(functools.partial(exchange_kernel, capacity, row_norm, lea...  143 us
    pallas_call x1, Pallas kernels, body(): pl.pallas_call(functools.partial(local_kernel, capacity), grid=(block_cou...  11.4 us
    pallas_call x1, Pallas kernels, body(): pl.pallas_call(basis_kernel, grid=(total_rows // tile,), in_specs=[pl.Blo...  8.08 us

profile of v1, /device:TPU:0, one launch (start us, length us, event | category | flops | bytes accessed | tf_op | source)
XLA Modules:
  0.0 164.2 jit_solution(7078155515673744754)
XLA Ops:
  0.6 11.4 %sketch_blocks.1 = (bf16[128,128,128]{2,1,0:T(8,128)(2,1)}, f32[8,128,384]{2,1,0:T(8,128)}) custom-call(s32[64]{0:T(128)} %map_ref.1, s32[64,128]{1,0:T(8,128)} %order_ref.1, bf16[8192,256]{1,0:T(8,128)(2,1)} %x_ref.1, bf16[256,128]{1,0:T(8,128)(2,1)} %sketch_ref.1), custom_call_target="tpu_custom_call" | custom-call | tf_op jit(solution)/shard_map/sketch_blocks/pallas_call | solution.py:296
  12.0 142.7 %exchange_and_merge.1 = (bf16[128,128,128]{2,1,0:T(8,128)(2,1)}, f32[128,128]{1,0:T(8,128)}, f32[3,128,128]{2,1,0:T(8,128)}, f32[128,256]{1,0:T(8,128)}) custom-call(bf16[128,128,128]{2,1,0:T(8,128)(2,1)} %get-tuple-element.9.packed_ref, f32[8,128,384]{2,1,0:T(8,128)} %get-tuple-element.10.sums_ref, f32[3,256,128]{2,1,0:T(8,128)} %level_ref.1), custom_call_target="tpu_custom_call" | custom-call | tf_op jit(solution)/shard_map/exchange_and_merge/pallas_call | solution.py:323
  154.7 0.0 copy-start
  154.7 0.0 copy-start.1
  154.7 8.1 %leaf_bases.1 = bf16[16384,128]{1,0:T(8,128)(2,1)} custom-call(bf16[16384,128]{1,0:T(8,128)(2,1)} %bitcast.3, f32[128,128]{1,0:T(8,128)} %get-tuple-element.12.inverse_ref), custom_call_target="tpu_custom_call" | custom-call | tf_op jit(solution)/shard_map/leaf_bases/pallas_call | solution.py:360
  162.8 0.0 copy-done
  162.8 0.7 copy.10
  163.5 0.0 copy-done.1
  163.5 0.7 copy.11
Async XLA Ops:
  154.7 8.1 %copy-start = (f32[3,128,128]{2,1,0:T(8,128)S(1)}, f32[3,128,128]{2,1,0:T(8,128)}, u32[]{:S(2)}) copy-start(f32[3,128,128]{2,1,0:T(8,128)} %get-tuple-element.13) | copy-start | bytes 589828
  154.7 8.8 %copy-start.1 = (f32[128,256]{1,0:T(8,128)S(1)}, f32[128,256]{1,0:T(8,128)}, u32[]{:S(2)}) copy-start(f32[128,256]{1,0:T(8,128)} %get-tuple-element.14) | copy-start | bytes 393220

commit v2 on v1

--- a/solution.py
+++ b/solution.py
@@ -12,6 +12,7 @@
 SHIFT = 0.01
 TILE = 8
 GROUP = 4
+SPLITS = 4
 STEP_BLOCKS = 8
 VMEM_BYTES = 56 * 1024 * 1024
 MESH = pl.DeviceIdType.MESH
@@ -44,37 +45,41 @@
     return jnp.where(rows == cols, 1.0, 0.0).astype(jnp.float32)
 
 
-def inverse_factor(gram):
+def inverse_factor(gram, between=None):
     size = gram.shape[0]
-    row_id = lax.broadcasted_iota(jnp.int32, (size, size), 0)
+    row_id = lax.broadcasted_iota(jnp.int32, (TILE, size), 0)
 
     def panel(_, carry):
         a, b = carry
+        first = jnp.zeros((TILE, size), jnp.float32)
         for s in range(0, TILE, GROUP):
             cols = [jnp.broadcast_to(a[:, s + j : s + j + 1], (size, size)) for j in range(GROUP)]
             rows_a = [a[s + j : s + j + 1, :] for j in range(GROUP)]
             rows_b = [b[s + j : s + j + 1, :] for j in range(GROUP)]
-            scales = []
             for j in range(GROUP):
-                pivot = cols[j][s + j : s + j + 1, :]
-                inv = 1.0 / pivot
-                scales.append(lax.rsqrt(pivot))
+                scale = lax.rsqrt(cols[j][s + j : s + j + 1, :])
+                inv = scale * scale
                 for i in range(j + 1, GROUP):
                     factor = cols[j][s + i : s + i + 1, :] * inv
                     cols[i] = cols[i] - cols[j] * factor
                     rows_a[i] = rows_a[i] - factor * rows_a[j]
                     rows_b[i] = rows_b[i] - factor * rows_b[j]
-                below = jnp.where(row_id > s + j, cols[j], 0.0)
+                top = jnp.where(row_id > s + j, cols[j][:TILE], 0.0)
+                below = jnp.concatenate([top, cols[j][TILE:]], axis=0)
                 a = a - below * (rows_a[j] * inv)
                 b = b - below * (rows_b[j] * inv)
-            for j in range(GROUP):
-                b = jnp.where(row_id == s + j, rows_b[j] * scales[j], b)
+                first = jnp.where(row_id == s + j, rows_b[j] * scale, first)
         a = jnp.concatenate([a[TILE:], jnp.zeros((TILE, size), jnp.float32)], axis=0)
         a = pltpu.roll(a, size - TILE, 1)
-        b = jnp.concatenate([b[TILE:], b[:TILE]], axis=0)
+        b = jnp.concatenate([b[TILE:], first], axis=0)
         return a, b
 
-    return lax.fori_loop(0, size // TILE, panel, (gram, identity(size)))[1]
+    def part(i, carry):
+        if between is not None:
+            between(i)
+        return lax.fori_loop(0, size // (TILE * SPLITS), panel, carry)
+
+    return lax.fori_loop(0, SPLITS, part, (gram, identity(size)))[1]
 
 
 def local_kernel(capacity, map_ref, order_ref, x_ref, sketch_ref, packed_ref, sums_ref, count_ref):
@@ -174,6 +179,35 @@
         copy.start()
         return copy
 
+    pieces = max(1, capacity // 4)
+    depth = capacity // pieces
+    chunks = (leaves - 1) * pieces
+    per = max(1, chunks // (5 + LEVELS + SPLITS * (LEVELS + 1)))
+    after_sums = 5 * per
+    first = chunks - per * (5 + LEVELS + SPLITS * (LEVELS + 1))
+
+    def chunk(i):
+        d = 1 + lax.rem(i, leaves - 1)
+        offset = lax.div(i, leaves - 1) * depth
+        peer = lax.rem(me + d, leaves)
+        return pltpu.make_async_remote_copy(
+            src_ref=packed_ref.at[pl.ds(peer * capacity + offset, depth)],
+            dst_ref=received_ref.at[pl.ds(me * capacity + offset, depth)],
+            send_sem=block_send.at[i],
+            recv_sem=block_recv.at[i],
+            device_id=(peer, line),
+            device_id_type=MESH,
+        )
+
+    def send_chunks(base, count):
+        def send(i, carry):
+            chunk(base + i).start()
+            return carry
+
+        lax.fori_loop(0, count, send, 0)
+
+    send_chunks(0, first)
+
     held, start, size = sums_ref, 0, rank
     for k in range(rounds):
         mask = 2**k
@@ -205,18 +239,7 @@
         sums.append(
             remote(held.at[peer], landed.at[me], leaf_send.at[d], leaf_recv.at[d], (peer, line))
         )
-    blocks = []
-    for d in sorted(range(1, leaves), key=lambda value: abs(value - leaves // 2)):
-        peer = lax.rem(me + d, leaves)
-        blocks.append(
-            remote(
-                packed_ref.at[pl.ds(peer * capacity, capacity)],
-                received_ref.at[pl.ds(me * capacity, capacity)],
-                block_send.at[d],
-                block_recv.at[d],
-                (peer, line),
-            )
-        )
+    send_chunks(first, after_sums)
     total = held[me]
     for d in range(1, leaves):
         sums[d - 1].wait()
@@ -237,7 +260,12 @@
         copy.wait()
 
     eye = identity(rank)
-    inverse = inverse_factor(whole[:, :rank] / row_norm + SHIFT * eye)
+    base = first + after_sums
+    inverse = inverse_factor(
+        whole[:, :rank] / row_norm + SHIFT * eye,
+        lambda i, base=base: send_chunks(base + i * per, per),
+    )
+    base += SPLITS * per
     inverse_ref[...] = inverse
     nodes[0] = jnp.dot(inverse, whole[:, rank:], precision=HIGHEST) * (
         math.sqrt(sample_cols) / row_norm
@@ -246,6 +274,8 @@
         copy = remote(
             nodes.at[t], siblings.at[t], node_send.at[t], node_recv.at[t], (flip(me, 2**t), line)
         )
+        send_chunks(base, per)
+        base += per
         own_node = nodes[t]
         sketch = level_ref[t]
         projected = jnp.dot(own_node, sketch, precision=HIGHEST)
@@ -256,7 +286,11 @@
         other = jnp.dot(other_node, sketch, precision=HIGHEST)
         other_wide = jnp.concatenate([other, other_node], axis=1)
         product = own_product + dot_first(other, other_wide, HIGHEST)
-        inverse = inverse_factor(product[:, :rank] / (2 * rank) + SHIFT * eye)
+        inverse = inverse_factor(
+            product[:, :rank] / (2 * rank) + SHIFT * eye,
+            lambda i, base=base: send_chunks(base + i * per, per),
+        )
+        base += SPLITS * per
         transfers_ref[t] = dot_last(projected, inverse, HIGHEST)
         parent = jnp.dot(inverse, product[:, rank:], precision=HIGHEST) * (
             math.sqrt(sample_cols) / (2 * rank)
@@ -267,16 +301,22 @@
             nodes[t + 1] = parent
 
     own.wait()
-    for copy in blocks:
-        copy.wait()
+
+    def finish(i, carry):
+        chunk(i).wait()
+        return carry
+
+    lax.fori_loop(0, chunks, finish, 0)
 
 
 def basis_kernel(rows_ref, inverse_ref, basis_ref):
     inverse = inverse_ref[...]
     upper = inverse.astype(jnp.bfloat16)
     lower = (inverse - upper.astype(jnp.float32)).astype(jnp.bfloat16)
+    both = jnp.concatenate([upper, lower], axis=1)
     rows = rows_ref[...]
-    basis_ref[...] = (dot_last(rows, upper) + dot_last(rows, lower)).astype(jnp.bfloat16)
+    twice = jnp.concatenate([rows, rows], axis=1)
+    basis_ref[...] = dot_last(twice, both).astype(jnp.bfloat16)
 
 
 def body(samples, row_order, cluster_map, leaf_sketch, level_sketch):
@@ -320,6 +360,7 @@
         pltpu.VMEM((leaves, rank >> (k + 1), width), jnp.float32) for k in range(rounds)
     ]
     dma = pltpu.SemaphoreType.DMA
+    chunks = (leaves - 1) * max(1, capacity // 4)
     received, inverse, transfers, summary = pl.pallas_call(
         functools.partial(exchange_kernel, capacity, row_norm, leaves, lines),
         in_specs=[anywhere, vmem, vmem],
@@ -337,8 +378,8 @@
             pltpu.VMEM((rank, width), jnp.float32),
             pltpu.VMEM((LEVELS, rank, sample_cols), jnp.float32),
             pltpu.VMEM((LEVELS, rank, sample_cols), jnp.float32),
-            dma((leaves,)),
-            dma((leaves,)),
+            dma((chunks,)),
+            dma((chunks,)),
             dma((rounds,)),
             dma((rounds,)),
             dma((leaves,)),

time: 165 us -> 147 us (0.89)
  Pallas kernels: 162 us -> 144 us
    pallas_call x1, Pallas kernels: 143 us -> 125 us  [body(): pl.pallas_call(functools.partial(exchange_kernel, capacity, row_norm, lea...]
where the time goes in v2:
time: 147 us; the launch traced here: 146 us
  Pallas kernels  144 us (98%)
    pallas_call x1, Pallas kernels, body(): pl.pallas_call(functools.partial(exchange_kernel, capacity, row_norm, lea...  125 us
    pallas_call x1, Pallas kernels, body(): pl.pallas_call(functools.partial(local_kernel, capacity), grid=(block_cou...  11.4 us
    pallas_call x1, Pallas kernels, body(): pl.pallas_call(basis_kernel, grid=(total_rows // tile,), in_specs=[pl.Blo...  8.07 us

profile of v2, /device:TPU:0, one launch (start us, length us, event | category | flops | bytes accessed | tf_op | source)
XLA Modules:
  0.0 146.5 jit_solution(7182825575863685416)
XLA Ops:
  0.6 11.4 %sketch_blocks.1 = (bf16[128,128,128]{2,1,0:T(8,128)(2,1)}, f32[8,128,384]{2,1,0:T(8,128)}) custom-call(s32[64]{0:T(128)} %map_ref.1, s32[64,128]{1,0:T(8,128)} %order_ref.1, bf16[8192,256]{1,0:T(8,128)(2,1)} %x_ref.1, bf16[256,128]{1,0:T(8,128)(2,1)} %sketch_ref.1), custom_call_target="tpu_custom_call" | custom-call | tf_op jit(solution)/shard_map/sketch_blocks/pallas_call | solution.py:336
  12.0 125.0 %exchange_and_merge.1 = (bf16[128,128,128]{2,1,0:T(8,128)(2,1)}, f32[128,128]{1,0:T(8,128)}, f32[3,128,128]{2,1,0:T(8,128)}, f32[128,256]{1,0:T(8,128)}) custom-call(bf16[128,128,128]{2,1,0:T(8,128)(2,1)} %get-tuple-element.9.packed_ref, f32[8,128,384]{2,1,0:T(8,128)} %get-tuple-element.10.sums_ref, f32[3,256,128]{2,1,0:T(8,128)} %level_ref.1), custom_call_target="tpu_custom_call" | custom-call | tf_op jit(solution)/shard_map/exchange_and_merge/pallas_call | solution.py:364
  137.0 0.0 copy-start
  137.0 0.0 copy-start.1
  137.1 8.1 %leaf_bases.1 = bf16[16384,128]{1,0:T(8,128)(2,1)} custom-call(bf16[16384,128]{1,0:T(8,128)(2,1)} %bitcast.3, f32[128,128]{1,0:T(8,128)} %get-tuple-element.12.inverse_ref), custom_call_target="tpu_custom_call" | custom-call | tf_op jit(solution)/shard_map/leaf_bases/pallas_call | solution.py:401
  145.1 0.0 copy-done
  145.1 0.7 copy.10
  145.8 0.0 copy-done.1
  145.8 0.7 copy.11
Async XLA Ops:
  137.0 8.1 %copy-start = (f32[3,128,128]{2,1,0:T(8,128)S(1)}, f32[3,128,128]{2,1,0:T(8,128)}, u32[]{:S(2)}) copy-start(f32[3,128,128]{2,1,0:T(8,128)} %get-tuple-element.13) | copy-start | bytes 589828
  137.0 8.8 %copy-start.1 = (f32[128,256]{1,0:T(8,128)S(1)}, f32[128,256]{1,0:T(8,128)}, u32[]{:S(2)}) copy-start(f32[128,256]{1,0:T(8,128)} %get-tuple-element.14) | copy-start | bytes 393220

commit v3 on v2

--- a/solution.py
+++ b/solution.py
@@ -14,6 +14,7 @@
 GROUP = 4
 SPLITS = 4
 STEP_BLOCKS = 8
+BASIS_PARTS = 16
 VMEM_BYTES = 56 * 1024 * 1024
 MESH = pl.DeviceIdType.MESH
 HIGHEST = lax.Precision.HIGHEST
@@ -82,35 +83,77 @@
     return lax.fori_loop(0, SPLITS, part, (gram, identity(size)))[1]
 
 
-def local_kernel(capacity, map_ref, order_ref, x_ref, sketch_ref, packed_ref, sums_ref, count_ref):
-    step = pl.program_id(0)
+def run(count, work):
+    def one(i, carry):
+        work(i)
+        return carry
+
+    lax.fori_loop(0, count, one, 0)
+
+
+def local_kernel(
+    capacity,
+    map_ref,
+    order_ref,
+    x_ref,
+    sketch_ref,
+    packed_ref,
+    sums_ref,
+    x_buf,
+    packed_buf,
+    sums_buf,
+    count_ref,
+    in_sem,
+    packed_sem,
+    sums_sem,
+):
     clusters = sums_ref.shape[0]
-    rows = order_ref.shape[1]
-
-    @pl.when(step == 0)
-    def _():
-        def clear(c, carry):
-            count_ref[c] = 0
-            sums_ref[c] = jnp.zeros(sums_ref.shape[1:], jnp.float32)
-            for j in range(capacity):
-                packed_ref[c * capacity + j] = jnp.zeros(packed_ref.shape[1:], jnp.bfloat16)
-            return carry
-
-        lax.fori_loop(0, clusters, clear, 0)
-
-    sketched = jnp.dot(x_ref[...], sketch_ref[...], preferred_element_type=jnp.float32).astype(
-        jnp.bfloat16
-    )
+    block_count, rows = order_ref.shape
+    tall = STEP_BLOCKS * rows
+
+    def load(step):
+        span = pl.ds(pl.multiple_of(step * tall, tall), tall)
+        return pltpu.make_async_copy(x_ref.at[span], x_buf.at[span], in_sem.at[step])
+
+    def store_packed(c):
+        span = pl.ds(c * capacity, capacity)
+        return pltpu.make_async_copy(packed_buf.at[span], packed_ref.at[span], packed_sem.at[c])
+
+    def store_sums(c):
+        return pltpu.make_async_copy(sums_buf.at[c], sums_ref.at[c], sums_sem.at[c])
+
+    def clear(c):
+        count_ref[c] = 0
+        sums_buf[c] = jnp.zeros(sums_buf.shape[1:], jnp.float32)
+        for j in range(capacity):
+            packed_buf[c * capacity + j] = jnp.zeros(packed_buf.shape[1:], jnp.bfloat16)
+
+    run(block_count // STEP_BLOCKS, lambda step: load(step).start())
+    run(clusters, clear)
     source = lax.broadcasted_iota(jnp.int32, (rows, rows), 0)
-    for i in range(STEP_BLOCKS):
-        cluster = map_ref[step * STEP_BLOCKS + i]
-        rank = count_ref[cluster]
-        count_ref[cluster] = rank + 1
-        block = sketched[i * rows : (i + 1) * rows]
-        taken = jnp.where(source == order_ref[i : i + 1, :], 1.0, 0.0).astype(jnp.bfloat16)
-        packed_ref[cluster * capacity + rank] = dot_first(taken, block).astype(jnp.bfloat16)
-        wide = jnp.concatenate([block, x_ref[i * rows : (i + 1) * rows, :]], axis=1)
-        sums_ref[cluster] += dot_first(block, wide)
+
+    def work(step):
+        load(step).wait()
+        x = x_buf[pl.ds(pl.multiple_of(step * tall, tall), tall), :]
+        order = order_ref[pl.ds(pl.multiple_of(step * STEP_BLOCKS, STEP_BLOCKS), STEP_BLOCKS), :]
+        sketched = jnp.dot(x, sketch_ref[...], preferred_element_type=jnp.float32).astype(
+            jnp.bfloat16
+        )
+        for i in range(STEP_BLOCKS):
+            cluster = map_ref[step * STEP_BLOCKS + i]
+            rank = count_ref[cluster]
+            count_ref[cluster] = rank + 1
+            block = sketched[i * rows : (i + 1) * rows]
+            taken = jnp.where(source == order[i : i + 1, :], 1.0, 0.0).astype(jnp.bfloat16)
+            packed_buf[cluster * capacity + rank] = dot_first(taken, block).astype(jnp.bfloat16)
+            wide = jnp.concatenate([block, x[i * rows : (i + 1) * rows, :]], axis=1)
+            sums_buf[cluster] += dot_first(block, wide)
+
+    run(block_count // STEP_BLOCKS, work)
+    run(clusters, lambda c: store_sums(c).start())
+    run(clusters, lambda c: store_packed(c).start())
+    run(clusters, lambda c: store_sums(c).wait())
+    run(clusters, lambda c: store_packed(c).wait())
 
 
 def flip(index, mask):
@@ -184,7 +227,7 @@
     chunks = (leaves - 1) * pieces
     per = max(1, chunks // (5 + LEVELS + SPLITS * (LEVELS + 1)))
     after_sums = 5 * per
-    first = chunks - per * (5 + LEVELS + SPLITS * (LEVELS + 1))
+    first = chunks - per * (4 + LEVELS + SPLITS * LEVELS)
 
     def chunk(i):
         d = 1 + lax.rem(i, leaves - 1)
@@ -200,11 +243,7 @@
         )
 
     def send_chunks(base, count):
-        def send(i, carry):
-            chunk(base + i).start()
-            return carry
-
-        lax.fori_loop(0, count, send, 0)
+        run(count, lambda i: chunk(base + i).start())
 
     send_chunks(0, first)
 
@@ -274,8 +313,10 @@
         copy = remote(
             nodes.at[t], siblings.at[t], node_send.at[t], node_recv.at[t], (flip(me, 2**t), line)
         )
-        send_chunks(base, per)
-        base += per
+        busy = t < LEVELS - 1
+        if busy:
+            send_chunks(base, per)
+            base += per
         own_node = nodes[t]
         sketch = level_ref[t]
         projected = jnp.dot(own_node, sketch, precision=HIGHEST)
@@ -288,7 +329,7 @@
         product = own_product + dot_first(other, other_wide, HIGHEST)
         inverse = inverse_factor(
             product[:, :rank] / (2 * rank) + SHIFT * eye,
-            lambda i, base=base: send_chunks(base + i * per, per),
+            (lambda i, base=base: send_chunks(base + i * per, per)) if busy else None,
         )
         base += SPLITS * per
         transfers_ref[t] = dot_last(projected, inverse, HIGHEST)
@@ -301,22 +342,38 @@
             nodes[t + 1] = parent
 
     own.wait()
-
-    def finish(i, carry):
-        chunk(i).wait()
-        return carry
-
-    lax.fori_loop(0, chunks, finish, 0)
-
-
-def basis_kernel(rows_ref, inverse_ref, basis_ref):
+    run(chunks, lambda i: chunk(i).wait())
+
+
+def basis_kernel(rows_ref, inverse_ref, basis_ref, in_buf, out_buf, in_sem, out_sem):
+    tall = rows_ref.shape[0] // BASIS_PARTS
+
+    def span(i):
+        return pl.ds(pl.multiple_of(i * tall, tall), tall)
+
+    def load(i):
+        return pltpu.make_async_copy(rows_ref.at[span(i)], in_buf.at[span(i)], in_sem.at[i])
+
+    def store(i):
+        return pltpu.make_async_copy(out_buf.at[span(i)], basis_ref.at[span(i)], out_sem.at[i])
+
+    run(BASIS_PARTS, lambda i: load(i).start())
     inverse = inverse_ref[...]
     upper = inverse.astype(jnp.bfloat16)
     lower = (inverse - upper.astype(jnp.float32)).astype(jnp.bfloat16)
-    both = jnp.concatenate([upper, lower], axis=1)
-    rows = rows_ref[...]
-    twice = jnp.concatenate([rows, rows], axis=1)
-    basis_ref[...] = dot_last(twice, both).astype(jnp.bfloat16)
+    both = jnp.concatenate([upper.T, lower.T], axis=0)
+
+    def work(i):
+        load(i).wait()
+        rows = in_buf[span(i), :]
+        twice = jnp.concatenate([rows, rows], axis=1)
+        out_buf[span(i), :] = jnp.dot(twice, both, preferred_element_type=jnp.float32).astype(
+            jnp.bfloat16
+        )
+        store(i).start()
+
+    run(BASIS_PARTS, work)
+    run(BASIS_PARTS, lambda i: store(i).wait())
 
 
 def body(samples, row_order, cluster_map, leaf_sketch, level_sketch):
@@ -332,25 +389,25 @@
     row_norm = float(lines * block_count * block_rows)
     vmem = pl.BlockSpec(memory_space=pltpu.VMEM)
     anywhere = pl.BlockSpec(memory_space=pl.ANY)
+    dma = pltpu.SemaphoreType.DMA
 
     packed, sums = pl.pallas_call(
         functools.partial(local_kernel, capacity),
-        grid=(block_count // STEP_BLOCKS,),
-        in_specs=[
-            pl.BlockSpec(memory_space=pltpu.SMEM),
-            pl.BlockSpec((STEP_BLOCKS, block_rows), lambda i: (i, 0)),
-            pl.BlockSpec((STEP_BLOCKS * block_rows, sample_cols), lambda i: (i, 0)),
-            pl.BlockSpec((sample_cols, rank), lambda i: (0, 0)),
-        ],
-        out_specs=[
-            pl.BlockSpec((slots, block_rows, rank), lambda i: (0, 0, 0)),
-            pl.BlockSpec((leaves, rank, width), lambda i: (0, 0, 0)),
-        ],
+        in_specs=[pl.BlockSpec(memory_space=pltpu.SMEM), vmem, anywhere, vmem],
+        out_specs=[anywhere, anywhere],
         out_shape=[
             jax.ShapeDtypeStruct((slots, block_rows, rank), jnp.bfloat16),
             jax.ShapeDtypeStruct((leaves, rank, width), jnp.float32),
         ],
-        scratch_shapes=[pltpu.SMEM((leaves,), jnp.int32)],
+        scratch_shapes=[
+            pltpu.VMEM((block_count * block_rows, sample_cols), jnp.bfloat16),
+            pltpu.VMEM((slots, block_rows, rank), jnp.bfloat16),
+            pltpu.VMEM((leaves, rank, width), jnp.float32),
+            pltpu.SMEM((leaves,), jnp.int32),
+            dma((block_count // STEP_BLOCKS,)),
+            dma((leaves,)),
+            dma((leaves,)),
+        ],
         compiler_params=pltpu.CompilerParams(vmem_limit_bytes=VMEM_BYTES),
         name="sketch_blocks",
     )(cluster_map, row_order, samples, leaf_sketch)
@@ -359,7 +416,6 @@
     shares = [
         pltpu.VMEM((leaves, rank >> (k + 1), width), jnp.float32) for k in range(rounds)
     ]
-    dma = pltpu.SemaphoreType.DMA
     chunks = (leaves - 1) * max(1, capacity // 4)
     received, inverse, transfers, summary = pl.pallas_call(
         functools.partial(exchange_kernel, capacity, row_norm, leaves, lines),
@@ -397,16 +453,17 @@
     )(packed, sums, level_sketch)
 
     total_rows = slots * block_rows
-    tile = min(2048, total_rows)
     basis = pl.pallas_call(
         basis_kernel,
-        grid=(total_rows // tile,),
-        in_specs=[
-            pl.BlockSpec((tile, rank), lambda i: (i, 0)),
-            pl.BlockSpec((rank, rank), lambda i: (0, 0)),
+        in_specs=[anywhere, vmem],
+        out_specs=anywhere,
+        out_shape=jax.ShapeDtypeStruct((total_rows, rank), jnp.bfloat16),
+        scratch_shapes=[
+            pltpu.VMEM((total_rows, rank), jnp.bfloat16),
+            pltpu.VMEM((total_rows, rank), jnp.bfloat16),
+            dma((BASIS_PARTS,)),
+            dma((BASIS_PARTS,)),
         ],
-        out_specs=pl.BlockSpec((tile, rank), lambda i: (i, 0)),
-        out_shape=jax.ShapeDtypeStruct((total_rows, rank), jnp.bfloat16),
         compiler_params=pltpu.CompilerParams(vmem_limit_bytes=VMEM_BYTES),
         name="leaf_bases",
     )(received.reshape(total_rows, rank), inverse)

time: 147 us -> 147 us (level)
  no operation moved by 1% of the time
where the time goes in v3:
time: 147 us; the launch traced here: 145 us
  Pallas kernels  143 us (97%)
    pallas_call x1, Pallas kernels, body(): pl.pallas_call(functools.partial(exchange_kernel, capacity, row_norm, lea...  125 us
    pallas_call x1, Pallas kernels, body(): pl.pallas_call(functools.partial(local_kernel, capacity), in_specs=[pl.Bl...  10.5 us
    pallas_call x1, Pallas kernels, body(): pl.pallas_call(basis_kernel, in_specs=[anywhere, vmem], out_specs=anywher...  7.61 us

profile of v3, /device:TPU:0, one launch (start us, length us, event | category | flops | bytes accessed | tf_op | source)
XLA Modules:
  0.0 145.3 jit_solution(5030372873234273538)
XLA Ops:
  0.6 10.5 %sketch_blocks.1 = (bf16[128,128,128]{2,1,0:T(8,128)(2,1)}, f32[8,128,384]{2,1,0:T(8,128)}) custom-call(s32[64]{0:T(128)} %map_ref.1, s32[64,128]{1,0:T(8,128)} %order_ref.1, bf16[8192,256]{1,0:T(8,128)(2,1)} %x_ref.1, bf16[256,128]{1,0:T(8,128)(2,1)} %sketch_ref.1), custom_call_target="tpu_custom_call" | custom-call | tf_op jit(solution)/shard_map/sketch_blocks/pallas_call | solution.py:394
  11.1 125.2 %exchange_and_merge.1 = (bf16[128,128,128]{2,1,0:T(8,128)(2,1)}, f32[128,128]{1,0:T(8,128)}, f32[3,128,128]{2,1,0:T(8,128)}, f32[128,256]{1,0:T(8,128)}) custom-call(bf16[128,128,128]{2,1,0:T(8,128)(2,1)} %get-tuple-element.9.packed_ref, f32[8,128,384]{2,1,0:T(8,128)} %get-tuple-element.10.sums_ref, f32[3,256,128]{2,1,0:T(8,128)} %level_ref.1), custom_call_target="tpu_custom_call" | custom-call | tf_op jit(solution)/shard_map/exchange_and_merge/pallas_call | solution.py:420
  136.4 0.0 copy-start
  136.4 0.0 copy-start.1
  136.4 7.6 %leaf_bases.1 = bf16[16384,128]{1,0:T(8,128)(2,1)} custom-call(bf16[16384,128]{1,0:T(8,128)(2,1)} %bitcast.3, f32[128,128]{1,0:T(8,128)} %get-tuple-element.12.inverse_ref), custom_call_target="tpu_custom_call" | custom-call | tf_op jit(solution)/shard_map/leaf_bases/pallas_call | solution.py:456
  144.0 0.0 copy-done
  144.0 0.7 copy.10
  144.7 0.0 copy-done.1
  144.7 0.7 copy.11
Async XLA Ops:
  136.4 7.6 %copy-start = (f32[3,128,128]{2,1,0:T(8,128)S(1)}, f32[3,128,128]{2,1,0:T(8,128)}, u32[]{:S(2)}) copy-start(f32[3,128,128]{2,1,0:T(8,128)} %get-tuple-element.13) | copy-start | bytes 589828
  136.4 8.3 %copy-start.1 = (f32[128,256]{1,0:T(8,128)S(1)}, f32[128,256]{1,0:T(8,128)}, u32[]{:S(2)}) copy-start(f32[128,256]{1,0:T(8,128)} %get-tuple-element.14) | copy-start | bytes 393220

commit v4 on v3

--- a/solution.py
+++ b/solution.py
@@ -83,6 +83,12 @@
     return lax.fori_loop(0, SPLITS, part, (gram, identity(size)))[1]
 
 
+def shares_of(capacity):
+    if capacity % 16:
+        return capacity, 0
+    return 3 * capacity // 4, 3 * capacity // 8
+
+
 def run(count, work):
     def one(i, carry):
         work(i)
@@ -99,6 +105,8 @@
     sketch_ref,
     packed_ref,
     sums_ref,
+    extra_ref,
+    table_ref,
     x_buf,
     packed_buf,
     sums_buf,
@@ -107,6 +115,7 @@
     packed_sem,
     sums_sem,
 ):
+    regular, spare = shares_of(capacity)
     clusters = sums_ref.shape[0]
     block_count, rows = order_ref.shape
     tall = STEP_BLOCKS * rows
@@ -130,6 +139,11 @@
 
     run(block_count // STEP_BLOCKS, lambda step: load(step).start())
     run(clusters, clear)
+    extra_ref[...] = jnp.zeros(extra_ref.shape, jnp.bfloat16)
+    table_row = lax.broadcasted_iota(jnp.int32, table_ref.shape, 0)
+    table_col = lax.broadcasted_iota(jnp.int32, table_ref.shape, 1)
+    table_ref[...] = jnp.where(table_row == 0, -1, 0)
+    count_ref[clusters] = 0
     source = lax.broadcasted_iota(jnp.int32, (rows, rows), 0)
 
     def work(step):
@@ -145,11 +159,23 @@
             count_ref[cluster] = rank + 1
             block = sketched[i * rows : (i + 1) * rows]
             taken = jnp.where(source == order[i : i + 1, :], 1.0, 0.0).astype(jnp.bfloat16)
-            packed_buf[cluster * capacity + rank] = dot_first(taken, block).astype(jnp.bfloat16)
+            slot = cluster * capacity + rank
+            moved = dot_first(taken, block).astype(jnp.bfloat16)
+            packed_buf[slot] = moved
+            if spare:
+                over = rank >= regular
+                seen = count_ref[clusters]
+                place = jnp.where(over, jnp.minimum(seen, spare), spare)
+                count_ref[clusters] = seen + jnp.where(over, 1, 0)
+                extra_ref[place] = moved
+                here = (table_row == 0) & (table_col == place) & (place < spare)
+                table_ref[...] = jnp.where(here, slot, table_ref[...])
             wide = jnp.concatenate([block, x[i * rows : (i + 1) * rows, :]], axis=1)
             sums_buf[cluster] += dot_first(block, wide)
 
     run(block_count // STEP_BLOCKS, work)
+    excess = jnp.where(count_ref[clusters] > spare, 1, 0)
+    table_ref[...] = jnp.where(table_row == 1, excess, table_ref[...])
     run(clusters, lambda c: store_sums(c).start())
     run(clusters, lambda c: store_packed(c).start())
     run(clusters, lambda c: store_sums(c).wait())
@@ -168,10 +194,15 @@
     packed_ref,
     sums_ref,
     level_ref,
+    extra_ref,
+    table_ref,
     received_ref,
     inverse_ref,
     transfers_ref,
     summary_ref,
+    extras_ref,
+    tables_ref,
+    excess_ref,
     *scratch,
 ):
     rounds = lines.bit_length() - 1
@@ -193,7 +224,15 @@
         node_send,
         node_recv,
         own_sem,
+        excesses,
+        table_send,
+        table_recv,
+        excess_send,
+        excess_recv,
+        extra_send,
+        extra_recv,
     ) = scratch[2 * rounds :]
+    regular, spare = shares_of(capacity)
     me = lax.axis_index("leaf")
     line = lax.axis_index("rows")
     rank = inverse_ref.shape[0]
@@ -222,12 +261,12 @@
         copy.start()
         return copy
 
-    pieces = max(1, capacity // 4)
-    depth = capacity // pieces
+    pieces = max(1, regular // 4)
+    depth = regular // pieces
     chunks = (leaves - 1) * pieces
     per = max(1, chunks // (5 + LEVELS + SPLITS * (LEVELS + 1)))
-    after_sums = 5 * per
-    first = chunks - per * (4 + LEVELS + SPLITS * LEVELS)
+    after_sums = 3 * per
+    first = chunks - per * (2 + LEVELS + SPLITS * LEVELS)
 
     def chunk(i):
         d = 1 + lax.rem(i, leaves - 1)
@@ -245,6 +284,35 @@
     def send_chunks(base, count):
         run(count, lambda i: chunk(base + i).start())
 
+    half = leaves // 2
+    mirror = lax.rem(me + half, leaves)
+    base_leaf = lax.div(me, half) * half
+    others = [base_leaf + lax.rem(me - base_leaf + d, half) for d in range(1, half)]
+    spares, tables = [], []
+    if spare:
+        stock = extra_ref.at[pl.ds(0, spare)]
+        crossing = remote(
+            stock, extras_ref.at[me], extra_send.at[0], extra_recv.at[0], (mirror, line)
+        )
+        for d, other in enumerate(others, 1):
+            spares.append(
+                remote(
+                    stock, extras_ref.at[me], extra_send.at[d], extra_recv.at[d], (other, line)
+                )
+            )
+        own_extra = pltpu.make_async_copy(stock, extras_ref.at[me], extra_send.at[2 * half])
+        own_extra.start()
+        tables_ref[me] = table_ref[...]
+        for d in range(1, leaves):
+            tables.append(
+                remote(
+                    table_ref,
+                    tables_ref.at[me],
+                    table_send.at[d],
+                    table_recv.at[d],
+                    (lax.rem(me + d, leaves), line),
+                )
+            )
     send_chunks(0, first)
 
     held, start, size = sums_ref, 0, rank
@@ -261,8 +329,8 @@
         )
         if k == 0:
             own = pltpu.make_async_copy(
-                packed_ref.at[pl.ds(me * capacity, capacity)],
-                received_ref.at[pl.ds(me * capacity, capacity)],
+                packed_ref.at[pl.ds(me * capacity, regular)],
+                received_ref.at[pl.ds(me * capacity, regular)],
                 own_sem,
             )
             own.start()
@@ -297,6 +365,18 @@
     ]
     for copy in shares:
         copy.wait()
+    if spare:
+        crossing.wait()
+        for d, other in enumerate(others, 1):
+            spares.append(
+                remote(
+                    extras_ref.at[mirror],
+                    extras_ref.at[mirror],
+                    extra_send.at[half + d],
+                    extra_recv.at[half + d],
+                    (other, line),
+                )
+            )
 
     eye = identity(rank)
     base = first + after_sums
@@ -341,6 +421,35 @@
         else:
             nodes[t + 1] = parent
 
+    if spare:
+        for copy in tables:
+            copy.wait()
+        excess = tables_ref[0]
+        for c in range(1, leaves):
+            excess = jnp.maximum(excess, tables_ref[c])
+        excesses[line] = excess
+        flags = [
+            remote(
+                excesses.at[line],
+                excesses.at[line],
+                excess_send.at[d],
+                excess_recv.at[d],
+                (me, lax.rem(line + d, lines)),
+            )
+            for d in range(1, lines)
+        ]
+        for copy in flags:
+            copy.wait()
+        excess = excesses[0]
+        for r in range(1, lines):
+            excess = jnp.maximum(excess, excesses[r])
+        excess_ref[...] = excess
+        own_extra.wait()
+        for copy in spares:
+            copy.wait()
+    else:
+        tables_ref[...] = jnp.zeros(tables_ref.shape, jnp.int32)
+        excess_ref[...] = jnp.zeros(excess_ref.shape, jnp.int32)
     own.wait()
     run(chunks, lambda i: chunk(i).wait())
 
@@ -374,6 +483,64 @@
 
     run(BASIS_PARTS, work)
     run(BASIS_PARTS, lambda i: store(i).wait())
+
+
+def spread_kernel(
+    capacity, tables_ref, rows_ref, extras_ref, inverse_ref, basis_ref, in_buf, out_buf,
+    in_sem, extra_sem, out_sem,
+):
+    regular, spare = shares_of(capacity)
+    me = lax.axis_index("leaf")
+    leaves = rows_ref.shape[0] // capacity
+    rows, rank = rows_ref.shape[1:]
+
+    def load(c):
+        span = pl.ds(c * capacity, regular)
+        return pltpu.make_async_copy(rows_ref.at[span], in_buf.at[span], in_sem.at[c])
+
+    def store(c):
+        span = pl.ds(c * capacity, capacity)
+        return pltpu.make_async_copy(out_buf.at[span], basis_ref.at[span], out_sem.at[c])
+
+    def patch(c, e, act):
+        slot = tables_ref[c, 0, e]
+
+        @pl.when((slot >= me * capacity) & (slot < (me + 1) * capacity))
+        def _():
+            act(
+                pltpu.make_async_copy(
+                    extras_ref.at[c, e],
+                    in_buf.at[c * capacity + slot - me * capacity],
+                    extra_sem.at[c, e],
+                )
+            )
+
+    run(leaves, lambda c: load(c).start())
+    inverse = inverse_ref[...]
+    upper = inverse.astype(jnp.bfloat16)
+    lower = (inverse - upper.astype(jnp.float32)).astype(jnp.bfloat16)
+    both = jnp.concatenate([upper.T, lower.T], axis=0)
+
+    def begin(c):
+        span = pl.ds(c * capacity + regular, capacity - regular)
+        in_buf[span] = jnp.zeros((capacity - regular, rows, rank), jnp.bfloat16)
+        for e in range(spare):
+            patch(c, e, lambda copy: copy.start())
+
+    run(leaves, begin)
+
+    def work(c):
+        load(c).wait()
+        for e in range(spare):
+            patch(c, e, lambda copy: copy.wait())
+        blocks = in_buf[pl.ds(c * capacity, capacity)].reshape(capacity * rows, rank)
+        twice = jnp.concatenate([blocks, blocks], axis=1)
+        bases = jnp.dot(twice, both, preferred_element_type=jnp.float32).astype(jnp.bfloat16)
+        out_buf[pl.ds(c * capacity, capacity)] = bases.reshape(capacity, rows, rank)
+        store(c).start()
+
+    run(leaves, work)
+    run(leaves, lambda c: store(c).wait())
 
 
 def body(samples, row_order, cluster_map, leaf_sketch, level_sketch):
@@ -391,19 +558,23 @@
     anywhere = pl.BlockSpec(memory_space=pl.ANY)
     dma = pltpu.SemaphoreType.DMA
 
-    packed, sums = pl.pallas_call(
+    regular, spare = shares_of(capacity)
+    table = jax.ShapeDtypeStruct((8, 128), jnp.int32)
+    packed, sums, extra, own_table = pl.pallas_call(
         functools.partial(local_kernel, capacity),
         in_specs=[pl.BlockSpec(memory_space=pltpu.SMEM), vmem, anywhere, vmem],
-        out_specs=[anywhere, anywhere],
+        out_specs=[anywhere, anywhere, vmem, vmem],
         out_shape=[
             jax.ShapeDtypeStruct((slots, block_rows, rank), jnp.bfloat16),
             jax.ShapeDtypeStruct((leaves, rank, width), jnp.float32),
+            jax.ShapeDtypeStruct((spare + 1, block_rows, rank), jnp.bfloat16),
+            table,
         ],
         scratch_shapes=[
             pltpu.VMEM((block_count * block_rows, sample_cols), jnp.bfloat16),
             pltpu.VMEM((slots, block_rows, rank), jnp.bfloat16),
             pltpu.VMEM((leaves, rank, width), jnp.float32),
-            pltpu.SMEM((leaves,), jnp.int32),
+            pltpu.SMEM((leaves + 1,), jnp.int32),
             dma((block_count // STEP_BLOCKS,)),
             dma((leaves,)),
             dma((leaves,)),
@@ -416,16 +587,19 @@
     shares = [
         pltpu.VMEM((leaves, rank >> (k + 1), width), jnp.float32) for k in range(rounds)
     ]
-    chunks = (leaves - 1) * max(1, capacity // 4)
-    received, inverse, transfers, summary = pl.pallas_call(
+    chunks = (leaves - 1) * max(1, regular // 4)
+    received, inverse, transfers, summary, extras, tables, excess = pl.pallas_call(
         functools.partial(exchange_kernel, capacity, row_norm, leaves, lines),
-        in_specs=[anywhere, vmem, vmem],
-        out_specs=[anywhere, vmem, vmem, vmem],
+        in_specs=[anywhere, vmem, vmem, anywhere, vmem],
+        out_specs=[anywhere, vmem, vmem, vmem, anywhere, vmem, vmem],
         out_shape=[
             jax.ShapeDtypeStruct((slots, block_rows, rank), jnp.bfloat16),
             jax.ShapeDtypeStruct((rank, rank), jnp.float32),
             jax.ShapeDtypeStruct((LEVELS, rank, rank), jnp.float32),
             jax.ShapeDtypeStruct((rank, sample_cols), jnp.float32),
+            jax.ShapeDtypeStruct((leaves, max(spare, 1), block_rows, rank), jnp.bfloat16),
+            jax.ShapeDtypeStruct((leaves, 8, 128), jnp.int32),
+            table,
         ],
         scratch_shapes=[
             *shares,
@@ -445,28 +619,62 @@
             dma((LEVELS,)),
             dma((LEVELS,)),
             dma,
+            pltpu.VMEM((lines, 8, 128), jnp.int32),
+            dma((leaves,)),
+            dma((leaves,)),
+            dma((lines,)),
+            dma((lines,)),
+            dma((leaves + 1,)),
+            dma((leaves + 1,)),
         ],
         compiler_params=pltpu.CompilerParams(
             collective_id=0, has_side_effects=True, vmem_limit_bytes=VMEM_BYTES
         ),
         name="exchange_and_merge",
-    )(packed, sums, level_sketch)
+    )(packed, sums, level_sketch, extra, own_table)
 
     total_rows = slots * block_rows
-    basis = pl.pallas_call(
-        basis_kernel,
-        in_specs=[anywhere, vmem],
-        out_specs=anywhere,
-        out_shape=jax.ShapeDtypeStruct((total_rows, rank), jnp.bfloat16),
-        scratch_shapes=[
-            pltpu.VMEM((total_rows, rank), jnp.bfloat16),
-            pltpu.VMEM((total_rows, rank), jnp.bfloat16),
-            dma((BASIS_PARTS,)),
-            dma((BASIS_PARTS,)),
-        ],
-        compiler_params=pltpu.CompilerParams(vmem_limit_bytes=VMEM_BYTES),
-        name="leaf_bases",
-    )(received.reshape(total_rows, rank), inverse)
+
+    def all_slots(full):
+        return pl.pallas_call(
+            basis_kernel,
+            in_specs=[anywhere, vmem],
+            out_specs=anywhere,
+            out_shape=jax.ShapeDtypeStruct((total_rows, rank), jnp.bfloat16),
+            scratch_shapes=[
+                pltpu.VMEM((total_rows, rank), jnp.bfloat16),
+                pltpu.VMEM((total_rows, rank), jnp.bfloat16),
+                dma((BASIS_PARTS,)),
+                dma((BASIS_PARTS,)),
+            ],
+            compiler_params=pltpu.CompilerParams(vmem_limit_bytes=VMEM_BYTES),
+            name="leaf_bases",
+        )(full.reshape(total_rows, rank), inverse)
+
+    def send_again():
+        return all_slots(lax.all_to_all(packed, "leaf", split_axis=0, concat_axis=0, tiled=True))
+
+    def spread():
+        return pl.pallas_call(
+            functools.partial(spread_kernel, capacity),
+            in_specs=[pl.BlockSpec(memory_space=pltpu.SMEM), anywhere, anywhere, vmem],
+            out_specs=anywhere,
+            out_shape=jax.ShapeDtypeStruct((slots, block_rows, rank), jnp.bfloat16),
+            scratch_shapes=[
+                pltpu.VMEM((slots, block_rows, rank), jnp.bfloat16),
+                pltpu.VMEM((slots, block_rows, rank), jnp.bfloat16),
+                dma((leaves,)),
+                dma((leaves, spare)),
+                dma((leaves,)),
+            ],
+            compiler_params=pltpu.CompilerParams(vmem_limit_bytes=VMEM_BYTES),
+            name="spread_bases",
+        )(tables, received, extras, inverse).reshape(total_rows, rank)
+
+    if spare:
+        basis = lax.cond(excess[1, 0] > 0, send_again, spread)
+    else:
+        basis = all_slots(received)
     return basis, transfers[None], summary[None]
 
 

time: 147 us -> 148 us (level)
  no operation moved by 1% of the time
where the time goes in v4:
time: 148 us; the launch traced here: 147 us
  Pallas kernels  143 us (97%)
  local copies, waits for them, and re-layouts  2.54 us (2%)
    pallas_call x1, Pallas kernels, body(): pl.pallas_call(functools.partial(exchange_kernel, capacity, row_norm, lea...  127 us
    pallas_call x1, Pallas kernels, body(): pl.pallas_call(functools.partial(local_kernel, capacity), in_specs=[pl.Bl...  9.85 us
    pallas_call x1, Pallas kernels, spread(): pl.pallas_call(functools.partial(spread_kernel, capacity), in_specs=[pl.B...  7.07 us

profile of v4, /device:TPU:0, one launch (start us, length us, event | category | flops | bytes accessed | tf_op | source)
XLA Modules:
  0.0 147.3 jit_solution(12808801962053900348)
XLA Ops:
  0.6 9.8 %sketch_blocks.1 = (bf16[128,128,128]{2,1,0:T(8,128)(2,1)S(1)}, f32[8,128,384]{2,1,0:T(8,128)}, bf16[7,128,128]{2,1,0:T(8,128)(2,1)}, s32[8,128]{1,0:T(8,128)}) custom-call(s32[64]{0:T(128)} %map_ref.1, s32[64,128]{1,0:T(8,128)} %order_ref.1, bf16[8192,256]{1,0:T(8,128)(2,1)} %x_ref.1, bf16[256,128]{1,0:T(8,128)(2,1)} %sketch_ref.1), custom_call_target="tpu_custom_call" | custom-call | tf_op jit(solution)/shard_map/sketch_blocks/pallas_call | solution.py:563
  10.5 126.5 %exchange_and_merge.1 = (bf16[128,128,128]{2,1,0:T(8,128)(2,1)}, f32[128,128]{1,0:T(8,128)S(1)}, f32[3,128,128]{2,1,0:T(8,128)}, f32[128,256]{1,0:T(8,128)}, bf1...) custom-call(bf16[128,128,128]{2,1,0:T(8,128)(2,1)S(1)} %get-tuple-element.35.packed_ref, ...), custom_call_target="tpu_custom_call" | custom-call | tf_op jit(solution)/shard_map/exchange_and_merge/pallas_call | solution.py:591
  137.0 1.2 slice.3
  138.9 0.0 copy-start
  138.9 0.0 copy-start.1
  138.9 7.1 %conditional.1 = (bf16[16384,128]{1,0:T(8,128)(2,1)}) conditional(s32[]{:T(128)} %bitcast.2, (s32[8,8,128]{2,1,0:T(8,128)S(1)}, bf16[128,128,128]{2,1,0:T(8,128)(2,1)}, bf16[8,6,128,128]{3,2,1,0:T(8,128)(2,1)S(1)}, f32[128,128]{1,0:T(8,128)S(1)}) %tuple.14, (bf16[128,128,128]{2,1,0:T(8,128)(2,1)S(1)}, f32[128,128]{1,0:T(8,128)S(1)}) %tuple.15), branch_computations={%region_0.0_spmd, %region_1.0_spmd} | conditional | bytes 8388616 | solution.py:675
  138.9 7.1 %spread_bases.1 = bf16[128,128,128]{2,1,0:T(8,128)(2,1)} custom-call(s32[8,8,128]{2,1,0:T(8,128)S(1)} %get-tuple-element.12.tables_ref, bf16[128,128,128]{2,1,0:T(8,128)(2,1)} %get-tuple-element.16.rows_ref, bf16[8,6,128,128]{3,2,1,0:T(8,128)(2,1)S(1)} %get-tuple-element.17.extras_ref, f32[128,128]{1,0:T(8,128)S(1)} %get-tuple-element.18.inverse_ref), custom_call_target="tpu_custom_call" | custom-call | tf_op jit(solution)/shard_map/cond/branch_0_fun/spread_bases/pallas_call | solution.py:658
  146.0 0.0 copy-done
  146.0 0.7 copy.12
  146.7 0.0 copy-done.1
  146.7 0.7 copy.13
Async XLA Ops:
  138.9 7.1 %copy-start = (f32[3,128,128]{2,1,0:T(8,128)S(1)}, f32[3,128,128]{2,1,0:T(8,128)}, u32[]{:S(2)}) copy-start(f32[3,128,128]{2,1,0:T(8,128)} %get-tuple-element.44) | copy-start | bytes 589828
  138.9 7.8 %copy-start.1 = (f32[128,256]{1,0:T(8,128)S(1)}, f32[128,256]{1,0:T(8,128)}, u32[]{:S(2)}) copy-start(f32[128,256]{1,0:T(8,128)} %get-tuple-element.45) | copy-start | bytes 393220

commit v5 on v4

--- a/solution.py
+++ b/solution.py
@@ -11,7 +11,6 @@
 LEVELS = 3
 SHIFT = 0.01
 TILE = 8
-GROUP = 4
 SPLITS = 4
 STEP_BLOCKS = 8
 BASIS_PARTS = 16
@@ -48,39 +47,53 @@
 
 def inverse_factor(gram, between=None):
     size = gram.shape[0]
+    part_rows = size // SPLITS
     row_id = lax.broadcasted_iota(jnp.int32, (TILE, size), 0)
-
-    def panel(_, carry):
-        a, b = carry
-        first = jnp.zeros((TILE, size), jnp.float32)
-        for s in range(0, TILE, GROUP):
-            cols = [jnp.broadcast_to(a[:, s + j : s + j + 1], (size, size)) for j in range(GROUP)]
-            rows_a = [a[s + j : s + j + 1, :] for j in range(GROUP)]
-            rows_b = [b[s + j : s + j + 1, :] for j in range(GROUP)]
-            for j in range(GROUP):
-                scale = lax.rsqrt(cols[j][s + j : s + j + 1, :])
-                inv = scale * scale
-                for i in range(j + 1, GROUP):
-                    factor = cols[j][s + i : s + i + 1, :] * inv
-                    cols[i] = cols[i] - cols[j] * factor
-                    rows_a[i] = rows_a[i] - factor * rows_a[j]
-                    rows_b[i] = rows_b[i] - factor * rows_b[j]
-                top = jnp.where(row_id > s + j, cols[j][:TILE], 0.0)
-                below = jnp.concatenate([top, cols[j][TILE:]], axis=0)
-                a = a - below * (rows_a[j] * inv)
-                b = b - below * (rows_b[j] * inv)
-                first = jnp.where(row_id == s + j, rows_b[j] * scale, first)
-        a = jnp.concatenate([a[TILE:], jnp.zeros((TILE, size), jnp.float32)], axis=0)
-        a = pltpu.roll(a, size - TILE, 1)
-        b = jnp.concatenate([b[TILE:], first], axis=0)
-        return a, b
-
-    def part(i, carry):
+    col_id = lax.broadcasted_iota(jnp.int32, (TILE, size), 1)
+    one_row = lax.broadcasted_iota(jnp.int32, (1, size), 1)
+    done = []
+    m = gram
+    for part in range(SPLITS):
         if between is not None:
-            between(i)
-        return lax.fori_loop(0, size // (TILE * SPLITS), panel, carry)
-
-    return lax.fori_loop(0, SPLITS, part, (gram, identity(size)))[1]
+            between(part)
+        live = size - part * part_rows
+        group = 2 if live > 96 else 4
+        keep_cols = lax.broadcasted_iota(jnp.int32, (live, size), 1)
+
+        def panel(i, m, part=part, live=live, group=group, keep_cols=keep_cols):
+            first = jnp.zeros((TILE, size), jnp.float32)
+            for s in range(0, TILE, group):
+                cols = [
+                    jnp.broadcast_to(m[:, s + j : s + j + 1], (live, size)) for j in range(group)
+                ]
+                inside = (one_row >= s) & (one_row < s + group)
+                rows = [
+                    jnp.where(inside, jnp.where(one_row == s + j, 1.0, 0.0), m[s + j : s + j + 1])
+                    for j in range(group)
+                ]
+                m = jnp.where((keep_cols >= s) & (keep_cols < s + group), 0.0, m)
+                for j in range(group):
+                    scale = lax.rsqrt(cols[j][s + j : s + j + 1, :])
+                    inv = scale * scale
+                    for k in range(j + 1, group):
+                        factor = cols[j][s + k : s + k + 1, :] * inv
+                        cols[k] = cols[k] - cols[j] * factor
+                        rows[k] = rows[k] - factor * rows[j]
+                    top = jnp.where(row_id > s + j, cols[j][:TILE], 0.0)
+                    below = jnp.concatenate([top, cols[j][TILE:]], axis=0)
+                    m = m - below * (rows[j] * inv)
+                    first = jnp.where(row_id == s + j, rows[j] * scale, first)
+            unused = size - TILE * (part * (part_rows // TILE) + i)
+            first = jnp.where((col_id > row_id) & (col_id < unused), 0.0, first)
+            m = jnp.concatenate([m[TILE:], first], axis=0)
+            return pltpu.roll(m, size - TILE, 1)
+
+        m = lax.fori_loop(0, part_rows // TILE, panel, m)
+        finished = m[live - part_rows :]
+        turned = (part + 1) * part_rows
+        done.append(pltpu.roll(finished, turned, 1) if turned < size else finished)
+        m = m[: live - part_rows]
+    return jnp.concatenate(done, axis=0)
 
 
 def shares_of(capacity):

time: 148 us -> 147 us (level)
  no operation moved by 1% of the time
where the time goes in v5:
time: 147 us; the launch traced here: 146 us
  Pallas kernels  143 us (97%)
  local copies, waits for them, and re-layouts  2.54 us (2%)
    pallas_call x1, Pallas kernels, body(): pl.pallas_call(functools.partial(exchange_kernel, capacity, row_norm, lea...  126 us
    pallas_call x1, Pallas kernels, body(): pl.pallas_call(functools.partial(local_kernel, capacity), in_specs=[pl.Bl...  9.85 us
    pallas_call x1, Pallas kernels, spread(): pl.pallas_call(functools.partial(spread_kernel, capacity), in_specs=[pl.B...  7.06 us

profile of v5, /device:TPU:0, one launch (start us, length us, event | category | flops | bytes accessed | tf_op | source)
XLA Modules:
  0.0 146.5 jit_solution(7013830436168105446)
XLA Ops:
  0.6 9.8 %sketch_blocks.1 = (bf16[128,128,128]{2,1,0:T(8,128)(2,1)S(1)}, f32[8,128,384]{2,1,0:T(8,128)}, bf16[7,128,128]{2,1,0:T(8,128)(2,1)}, s32[8,128]{1,0:T(8,128)}) custom-call(s32[64]{0:T(128)} %map_ref.1, s32[64,128]{1,0:T(8,128)} %order_ref.1, bf16[8192,256]{1,0:T(8,128)(2,1)} %x_ref.1, bf16[256,128]{1,0:T(8,128)(2,1)} %sketch_ref.1), custom_call_target="tpu_custom_call" | custom-call | tf_op jit(solution)/shard_map/sketch_blocks/pallas_call | solution.py:576
  10.5 125.7 %exchange_and_merge.1 = (bf16[128,128,128]{2,1,0:T(8,128)(2,1)}, f32[128,128]{1,0:T(8,128)S(1)}, f32[3,128,128]{2,1,0:T(8,128)}, f32[128,256]{1,0:T(8,128)}, bf1...) custom-call(bf16[128,128,128]{2,1,0:T(8,128)(2,1)S(1)} %get-tuple-element.35.packed_ref, ...), custom_call_target="tpu_custom_call" | custom-call | tf_op jit(solution)/shard_map/exchange_and_merge/pallas_call | solution.py:604
  136.2 1.2 slice.3
  138.0 0.0 copy-start
  138.1 0.0 copy-start.1
  138.1 7.1 %conditional.1 = (bf16[16384,128]{1,0:T(8,128)(2,1)}) conditional(s32[]{:T(128)} %bitcast.2, (s32[8,8,128]{2,1,0:T(8,128)S(1)}, bf16[128,128,128]{2,1,0:T(8,128)(2,1)}, bf16[8,6,128,128]{3,2,1,0:T(8,128)(2,1)S(1)}, f32[128,128]{1,0:T(8,128)S(1)}) %tuple.14, (bf16[128,128,128]{2,1,0:T(8,128)(2,1)S(1)}, f32[128,128]{1,0:T(8,128)S(1)}) %tuple.15), branch_computations={%region_0.0_spmd, %region_1.0_spmd} | conditional | bytes 8388616 | solution.py:688
  138.1 7.1 %spread_bases.1 = bf16[128,128,128]{2,1,0:T(8,128)(2,1)} custom-call(s32[8,8,128]{2,1,0:T(8,128)S(1)} %get-tuple-element.12.tables_ref, bf16[128,128,128]{2,1,0:T(8,128)(2,1)} %get-tuple-element.16.rows_ref, bf16[8,6,128,128]{3,2,1,0:T(8,128)(2,1)S(1)} %get-tuple-element.17.extras_ref, f32[128,128]{1,0:T(8,128)S(1)} %get-tuple-element.18.inverse_ref), custom_call_target="tpu_custom_call" | custom-call | tf_op jit(solution)/shard_map/cond/branch_0_fun/spread_bases/pallas_call | solution.py:671
  145.1 0.0 copy-done
  145.2 0.7 copy.12
  145.8 0.0 copy-done.1
  145.8 0.7 copy.13
Async XLA Ops:
  138.0 7.1 %copy-start = (f32[3,128,128]{2,1,0:T(8,128)S(1)}, f32[3,128,128]{2,1,0:T(8,128)}, u32[]{:S(2)}) copy-start(f32[3,128,128]{2,1,0:T(8,128)} %get-tuple-element.44) | copy-start | bytes 589828
  138.1 7.8 %copy-start.1 = (f32[128,256]{1,0:T(8,128)S(1)}, f32[128,256]{1,0:T(8,128)}, u32[]{:S(2)}) copy-start(f32[128,256]{1,0:T(8,128)} %get-tuple-element.45) | copy-start | bytes 393220

commit v6 on v5

--- a/solution.py
+++ b/solution.py
@@ -277,9 +277,8 @@
     pieces = max(1, regular // 4)
     depth = regular // pieces
     chunks = (leaves - 1) * pieces
-    per = max(1, chunks // (5 + LEVELS + SPLITS * (LEVELS + 1)))
-    after_sums = 3 * per
-    first = chunks - per * (2 + LEVELS + SPLITS * LEVELS)
+    per = max(1, chunks // 21)
+    first = min(chunks, 4 * per)
 
     def chunk(i):
         d = 1 + lax.rem(i, leaves - 1)
@@ -295,6 +294,8 @@
         )
 
     def send_chunks(base, count):
+        if count == 0:
+            return
         run(count, lambda i: chunk(base + i).start())
 
     half = leaves // 2
@@ -359,7 +360,6 @@
         sums.append(
             remote(held.at[peer], landed.at[me], leaf_send.at[d], leaf_recv.at[d], (peer, line))
         )
-    send_chunks(first, after_sums)
     total = held[me]
     for d in range(1, leaves):
         sums[d - 1].wait()
@@ -392,12 +392,12 @@
             )
 
     eye = identity(rank)
-    base = first + after_sums
+    base = first
     inverse = inverse_factor(
         whole[:, :rank] / row_norm + SHIFT * eye,
-        lambda i, base=base: send_chunks(base + i * per, per),
+        lambda i, base=base: send_chunks(base + i * per, per if i < 3 else 0),
     )
-    base += SPLITS * per
+    base += 3 * per
     inverse_ref[...] = inverse
     nodes[0] = jnp.dot(inverse, whole[:, rank:], precision=HIGHEST) * (
         math.sqrt(sample_cols) / row_norm
@@ -406,25 +406,24 @@
         copy = remote(
             nodes.at[t], siblings.at[t], node_send.at[t], node_recv.at[t], (flip(me, 2**t), line)
         )
-        busy = t < LEVELS - 1
-        if busy:
-            send_chunks(base, per)
-            base += per
         own_node = nodes[t]
         sketch = level_ref[t]
         projected = jnp.dot(own_node, sketch, precision=HIGHEST)
         wide = jnp.concatenate([projected, own_node], axis=1)
         own_product = dot_first(projected, wide, HIGHEST)
         copy.wait()
+        if t == LEVELS - 1:
+            send_chunks(base, chunks - base)
+        parts = (3, 2, 0)[t]
         other_node = siblings[t]
         other = jnp.dot(other_node, sketch, precision=HIGHEST)
         other_wide = jnp.concatenate([other, other_node], axis=1)
         product = own_product + dot_first(other, other_wide, HIGHEST)
         inverse = inverse_factor(
             product[:, :rank] / (2 * rank) + SHIFT * eye,
-            (lambda i, base=base: send_chunks(base + i * per, per)) if busy else None,
-        )
-        base += SPLITS * per
+            lambda i, base=base, parts=parts: send_chunks(base + i * per, per if i < parts else 0),
+        )
+        base += parts * per
         transfers_ref[t] = dot_last(projected, inverse, HIGHEST)
         parent = jnp.dot(inverse, product[:, rank:], precision=HIGHEST) * (
             math.sqrt(sample_cols) / (2 * rank)

time: 147 us -> 146 us (level)
  the two profiles are of different devices: /device:TPU:0 before, /device:TPU:12 now
where the time goes in v6:
time: 146 us; the launch traced here: 145 us
  Pallas kernels  142 us (97%)
  local copies, waits for them, and re-layouts  2.54 us (2%)
    pallas_call x1, Pallas kernels, body(): pl.pallas_call(functools.partial(exchange_kernel, capacity, row_norm, lea...  125 us
    pallas_call x1, Pallas kernels, body(): pl.pallas_call(functools.partial(local_kernel, capacity), in_specs=[pl.Bl...  9.85 us
    pallas_call x1, Pallas kernels, spread(): pl.pallas_call(functools.partial(spread_kernel, capacity), in_specs=[pl.B...  7.06 us

profile of v6, /device:TPU:12, one launch (start us, length us, event | category | flops | bytes accessed | tf_op | source)
XLA Modules:
  0.0 145.4 jit_solution(1972550356147856934)
XLA Ops:
  0.6 9.9 %sketch_blocks.1 = (bf16[128,128,128]{2,1,0:T(8,128)(2,1)S(1)}, f32[8,128,384]{2,1,0:T(8,128)}, bf16[7,128,128]{2,1,0:T(8,128)(2,1)}, s32[8,128]{1,0:T(8,128)}) custom-call(s32[64]{0:T(128)} %map_ref.1, s32[64,128]{1,0:T(8,128)} %order_ref.1, bf16[8192,256]{1,0:T(8,128)(2,1)} %x_ref.1, bf16[256,128]{1,0:T(8,128)(2,1)} %sketch_ref.1), custom_call_target="tpu_custom_call" | custom-call | tf_op jit(solution)/shard_map/sketch_blocks/pallas_call | solution.py:575
  10.5 124.6 %exchange_and_merge.1 = (bf16[128,128,128]{2,1,0:T(8,128)(2,1)}, f32[128,128]{1,0:T(8,128)S(1)}, f32[3,128,128]{2,1,0:T(8,128)}, f32[128,256]{1,0:T(8,128)}, bf1...) custom-call(bf16[128,128,128]{2,1,0:T(8,128)(2,1)S(1)} %get-tuple-element.35.packed_ref, ...), custom_call_target="tpu_custom_call" | custom-call | tf_op jit(solution)/shard_map/exchange_and_merge/pallas_call | solution.py:603
  135.1 1.2 slice.3
  137.0 0.0 copy-start
  137.0 0.0 copy-start.1
  137.0 7.1 %conditional.1 = (bf16[16384,128]{1,0:T(8,128)(2,1)}) conditional(s32[]{:T(128)} %bitcast.2, (s32[8,8,128]{2,1,0:T(8,128)S(1)}, bf16[128,128,128]{2,1,0:T(8,128)(2,1)}, bf16[8,6,128,128]{3,2,1,0:T(8,128)(2,1)S(1)}, f32[128,128]{1,0:T(8,128)S(1)}) %tuple.14, (bf16[128,128,128]{2,1,0:T(8,128)(2,1)S(1)}, f32[128,128]{1,0:T(8,128)S(1)}) %tuple.15), branch_computations={%region_0.0_spmd, %region_1.0_spmd} | conditional | bytes 8388616 | solution.py:687
  137.0 7.1 %spread_bases.1 = bf16[128,128,128]{2,1,0:T(8,128)(2,1)} custom-call(s32[8,8,128]{2,1,0:T(8,128)S(1)} %get-tuple-element.12.tables_ref, bf16[128,128,128]{2,1,0:T(8,128)(2,1)} %get-tuple-element.16.rows_ref, bf16[8,6,128,128]{3,2,1,0:T(8,128)(2,1)S(1)} %get-tuple-element.17.extras_ref, f32[128,128]{1,0:T(8,128)S(1)} %get-tuple-element.18.inverse_ref), custom_call_target="tpu_custom_call" | custom-call | tf_op jit(solution)/shard_map/cond/branch_0_fun/spread_bases/pallas_call | solution.py:670
  144.1 0.0 copy-done
  144.1 0.7 copy.12
  144.8 0.0 copy-done.1
  144.8 0.7 copy.13
Async XLA Ops:
  137.0 7.1 %copy-start = (f32[3,128,128]{2,1,0:T(8,128)S(1)}, f32[3,128,128]{2,1,0:T(8,128)}, u32[]{:S(2)}) copy-start(f32[3,128,128]{2,1,0:T(8,128)} %get-tuple-element.44) | copy-start | bytes 589828
  137.0 7.8 %copy-start.1 = (f32[128,256]{1,0:T(8,128)S(1)}, f32[128,256]{1,0:T(8,128)}, u32[]{:S(2)}) copy-start(f32[128,256]{1,0:T(8,128)} %get-tuple-element.45) | copy-start | bytes 393220
